TPU v7x, 256 devices: a whole 4x4x8 slice. The times are simulated.
256 devices in a mesh: gx: 8 (over y, x_lo), gy: 4 (over x_hi, core), gz: 8 (over z).
Axes of the slice: x: 4 (x_hi: 2, x_lo: 2; x = x_hi * 2 + x_lo), y: 4, z: 8, core: 2. Of those that a mesh axis runs over, the one named last changes fastest.
Arguments:
- positions: float32 [3, 32, 16, 16, 16], P(None, 'gx', 'gy', 'gz'), may hold values from 0 to 5
- occupancy: int32 [32, 16, 16], P('gx', 'gy', 'gz'), may hold values from 1 to 16
- neighbours: int32 [32, 16, 16, 16, 64], P('gx', 'gy', 'gz'), may hold values from 0 to 431
- edge_counts: int32 [32, 16, 16, 16], P('gx', 'gy', 'gz'), may hold values from 1 to 64
- atom_features: bfloat16 [32, 16, 16, 16, 128], P('gx', 'gy', 'gz'), may hold values from -6 to 6
- w_atom: bfloat16 [128, 128], replicated, may hold values from -0.5 to 0.5
- w_radial: bfloat16 [8, 128], replicated, may hold values from -2 to 2
- w_hidden: bfloat16 [128, 128], replicated, may hold values from -0.5 to 0.5
- w_tensor: bfloat16 [128, 32], replicated, may hold values from -0.5 to 0.5
- w_mix: bfloat16 [224, 128], replicated, may hold values from -0.375 to 0.375
- w_out: float32 [128], replicated, may hold values from -0.5 to 0.5
Outputs:
- atom_energy: float32 [32, 16, 16, 16], P('gx', 'gy', 'gz')
- forces: float32 [3, 32, 16, 16, 16], P(None, 'gx', 'gy', 'gz')
Inputs may be any that keep to these rules, and one draw needn't show every extreme that they name: `neighbours`: code 16 * 13 + s names the atom itself; other codes name the 26 neighbouring cell bins.
All inputs are finite; a program needn't handle non-finite values.
Results may differ from a plain program's by a relative error of at most 0.0075.
Values may be sent and summed in bfloat16 or wider, within the bound.
A program may use at most 128 MiB of HBM per device.

v0:
```python
import numpy as np
import jax
import jax.numpy as jnp
from jax import lax
from jax.experimental import pallas as pl
from jax.experimental.pallas import tpu as pltpu
from jax.sharding import PartitionSpec as P

F32 = jnp.float32
BF = jnp.bfloat16
root_three = 1.7320508075688772
L = 256
G = 2
CX, CY, CZ = 4, 4, 2
CELLS = 32
MAXCH = CELLS * (1024 // L) + G


def nn(a, b):
    return lax.dot_general(a, b, (((1,), (0,)), ((), ())), preferred_element_type=F32)


def nt(a, b):
    return lax.dot_general(a, b, (((1,), (1,)), ((), ())), preferred_element_type=F32)


def iota(shape, dim, dtype=jnp.int32):
    return lax.broadcasted_iota(jnp.int32, shape, dim).astype(dtype)


def onoff(mask):
    return jnp.where(mask, 1.0, 0.0).astype(F32)


def eye(n, m):
    return onoff(iota((n, m), 0) == iota((n, m), 1)).astype(BF)


def silu_both(x):
    sg = 0.5 * jnp.tanh(0.5 * x) + 0.5
    y = x * sg
    return y, sg + y - y * sg


def edge_kernel(
    occ_s, feats, rows, neigh, counts, w_atom, w_rad, w_hid, w_ten, w_mix, w_out, fold,
    energy_out, force_out,
    list_c, list_r, rank_sc, att_sc, rt_sc, ctr_sc, w_atomT, w_hidT, w_mixT, w_radpad, w_radrow, wout_b, c_sc,
    q_sc, dm_sc, m_sc, dq_sc, f_sc, en_sc, sec_sc, d1_sc, d2_sc, g_sc, ys_sc, geo_sc, eps_sc,
):
    ident = eye(128, 128)
    w_atomT[...] = nt(ident, w_atom[...]).astype(BF)
    w_hidT[...] = nt(ident, w_hid[...]).astype(BF)
    w_mixT[...] = nt(ident, w_mix[0:128, :]).astype(BF)
    w_radrow[...] = jnp.zeros((128, 128), BF)
    w_radrow[48:64, :] = jnp.concatenate([w_rad[...].astype(F32), jnp.zeros((8, 128), F32)], axis=0).astype(BF)
    w_radpad[...] = nt(ident, w_radrow[...])
    wout_b[...] = jnp.sum(
        jnp.where(iota((128, 128), 0) == iota((128, 128), 1), w_out[...], 0.0), axis=1, keepdims=True
    ) * jnp.ones((128, 128), F32)
    tail = w_mix[128:224, :]
    for l in range(3):
        sel = onoff(iota((32, 96), 1) == 3 * iota((32, 96), 0) + l).astype(BF)
        spread = nn(w_ten[...], sel).astype(BF)
        c_sc[l] = (0.125 * nn(spread, tail)).astype(BF)

    counts_t = nt(eye(16, 16), counts[...].astype(F32).astype(BF))
    lane64 = iota((8, 128), 1)
    low = lane64 < 64
    k_of = jnp.where(low, lane64, lane64 - 64)
    s_of = jnp.where(low, iota((8, 128), 0), iota((8, 128), 0) + 8)
    masks = []
    for c in range(CELLS):
        x, y, z = c // (CY * CZ), c // CZ % CY, c % CZ
        nb = jnp.concatenate([neigh[c, 0:8, :], neigh[c, 8:16, :]], axis=1)
        cnt = jnp.where(low, counts_t[0:8, c : c + 1], counts_t[8:16, c : c + 1]).astype(jnp.int32)
        code = lax.shift_right_logical(nb, 4)
        slot = lax.bitwise_and(nb, 15)
        occ_n = jnp.zeros((8, 128), jnp.int32)
        for k in range(27):
            at = ((x + k // 9) * 6 + y + k // 3 % 3) * 4 + z + k % 3
            occ_n = jnp.where(code == k, occ_s[at], occ_n)
        own = occ_s[((x + 1) * 6 + y + 1) * 4 + z + 1]
        live = (k_of < cnt) & (slot < occ_n) & (s_of < own) & (nb != 208 + s_of)
        masks.append(onoff(live))
        sub = iota((16, 128), 0)
        code_f, slot_f, s_f = code.astype(F32), slot.astype(F32), s_of.astype(F32)
        for i in range(8):
            a = jnp.where(
                sub == 0,
                code_f[i : i + 1],
                jnp.where(sub == 1, slot_f[i : i + 1], jnp.where(sub == 2, s_f[i : i + 1], jnp.where(sub == 3, 1.0, 0.0))),
            )
            att_sc[c, :, i * 128 : (i + 1) * 128] = a.astype(BF)
    mask = jnp.concatenate(masks, axis=0)
    mask_b = mask.astype(BF)
    upto = nn(mask_b, onoff(iota((128, 128), 0) <= iota((128, 128), 1)).astype(BF))
    total = nn(mask_b, jnp.ones((128, 128), BF))
    ri, ci = iota((256, 256), 0), iota((256, 256), 1)
    before = onoff((lax.shift_right_logical(ri, 3) == lax.shift_right_logical(ci, 3)) & (ci < ri)).astype(BF)
    base = nn(before, total.astype(BF))
    rank_sc[...] = jnp.where(mask > 0.5, upto - 1.0 + base, -1.0).astype(jnp.int32).reshape(CELLS, 8, 128)
    ends = base + total
    pos = jnp.int32(0)
    for c in range(CELLS):
        n_c = jnp.max(ends[8 * c + 7 : 8 * c + 8, :]).astype(jnp.int32)
        chunks = lax.div(n_c + (L - 1), L)

        def put(k, _, pos=pos, c=c):
            list_c[pos + k] = c
            list_r[pos + k] = k * L
            return 0

        lax.fori_loop(0, chunks, put, 0)
        pos = pos + chunks
    for i in range(G):
        list_c[pos + i] = 0
        list_r[pos + i] = 4096
    groups = lax.div(pos + (G - 1), G)

    lane = iota((32, 128), 1)
    code_i = iota((32, 128), 0)
    ca = code_i // 9
    cb = code_i // 3 - 3 * ca
    cc = code_i - 3 * (code_i // 3)
    coord = lax.shift_right_logical(lane, 4)
    step = jnp.where(coord == 0, ca, jnp.where(coord == 1, cb, jnp.where(coord == 2, cc, 1))) - 1
    shift = 5.0 * step.astype(F32)
    for c in range(CELLS):
        x, y, z = c // (CY * CZ), c // CZ % CY, c % CZ
        parts = []
        for k in range(0, 27, 3):
            at = ((x + k // 9) * 6 + y + k // 3 % 3) * 4 + z
            parts.append(rows[at : at + 3, :])
        parts.append(jnp.zeros((5, 128), F32))
        r27 = jnp.concatenate(parts, axis=0) + shift
        hi = r27.astype(BF)
        rest = r27 - hi.astype(F32)
        mid = rest.astype(BF)
        lo = (rest - mid.astype(F32)).astype(BF)
        cat = jnp.concatenate([hi, mid, lo, jnp.zeros((32, 128), BF)], axis=0)
        rt = nt(eye(64, 128), cat)
        rt_sc[c] = rt.astype(BF)
        centre = rt[:, 13:14] + (rt[:, 45:46] + rt[:, 77:78])
        ctr_sc[c] = centre * jnp.ones((64, L), F32)

    q_sc[...] = jnp.zeros_like(q_sc)
    dm_sc[...] = jnp.zeros_like(dm_sc)
    f_sc[...] = jnp.zeros_like(f_sc)
    en_sc[...] = jnp.zeros_like(en_sc)

    sub16 = iota((16, L), 0, F32)

    def where_of(c):
        x = lax.div(c, CY * CZ)
        rest = c - x * (CY * CZ)
        y = lax.div(rest, CZ)
        return x, y, rest - y * CZ

    def sphere(rx, ry, rz):
        d2 = rx * rx + ry * ry + rz * rz + 0.01
        inv = lax.rsqrt(d2)
        return d2, inv, d2 * inv, rx * inv, ry * inv, rz * inv

    def front(gi, _):
        ids = [gi * G + i for i in range(G)]
        cells = [list_c[i] for i in ids]
        atts, tabs = [], []
        for i, c in zip(ids, cells):
            rk = rank_sc[c]
            target = iota((L, 128), 0) + list_r[i]
            p = jnp.concatenate([onoff(rk[j : j + 1, :] == target).astype(BF) for j in range(8)], axis=1)
            atts.append(nt(att_sc[c], p))
        for c in cells:
            x, y, z = where_of(c)
            parts = [
                feats[pl.ds(((x + k // 3) * 6 + y + k % 3) * 4 + z, 3)].reshape(48, 128) for k in range(9)
            ]
            parts.append(jnp.zeros((80, 128), BF))
            t = nt(w_atomT[...], jnp.concatenate(parts, axis=0))
            tabs.append(
                jnp.concatenate([t[:, 0:384].astype(BF), (t[:, 384:512].astype(BF).astype(F32) + w_radpad[...]).astype(BF)], axis=1)
            )
        pres, rest = [], []
        for i, c, att, tab in zip(ids, cells, atts, tabs):
            code, slot, s, live = att[0:1], att[1:2], att[2:3], att[3:4]
            oh27 = onoff(code == iota((32, L), 0, F32)).astype(BF)
            m_slot = slot == sub16
            m_s = s == sub16
            got = nn(rt_sc[c], jnp.concatenate([oh27, oh27, oh27, jnp.zeros((32, L), BF)], axis=0))
            mine = ctr_sc[c]
            rel = []
            for d in range(3):
                sl = slice(16 * d, 16 * d + 16)
                rel.append(
                    jnp.sum(jnp.where(m_slot, got[sl], 0.0) - jnp.where(m_s, mine[sl], 0.0), axis=0, keepdims=True)
                )
            rx, ry, rz = rel
            d2, inv, dist, nx, ny, nz = sphere(rx, ry, rz)
            u = jnp.maximum(1.0 - d2 * (1.0 / 144.0), 0.0)
            w = live * (u * u)
            arg = (dist - (0.5 + 2.0 * iota((8, L), 0, F32))) * 0.5
            basis = jnp.exp(-(arg * arg))
            idx = code * 16.0 + slot
            oh = onoff(idx == iota((432, L), 0, F32))
            oh = jnp.concatenate(
                [oh[0:208], oh[208:224] + onoff(m_s), oh[224:432], basis, jnp.zeros((72, L), F32)], axis=0
            ).astype(BF)
            pres.append(nn(tab, oh))
            ylist = [
                jnp.ones((1, L), F32), nx, ny, nz, root_three * nx * ny, root_three * ny * nz,
                0.5 * (3.0 * nz * nz - 1.0), root_three * nx * nz, (0.5 * root_three) * (nx * nx - ny * ny),
            ]
            ys = jnp.concatenate([jnp.where(m_s, v, 0.0) for v in ylist], axis=0).astype(BF)
            geo = jnp.concatenate([rx, ry, rz, live, code, slot, s, w], axis=0)
            rest.append((ys, geo, w))
        firsts = [silu_both(v) for v in pres]
        secs = [silu_both(nn(w_hidT[...], f.astype(BF))) for f, _ in firsts]
        qs = []
        for (sec, d), (ys, geo, w) in zip(secs, rest):
            sb = sec.astype(BF)
            qs.append((sb, nt(ys, (sb.astype(F32) * w).astype(BF))))
        for i, c, (f, d1), (sec, d2), (ys, geo, w), (sb, q) in zip(ids, cells, firsts, secs, rest, qs):
            sec_sc[i] = sb
            d1_sc[i] = d1.astype(BF)
            d2_sc[i] = d2.astype(BF)
            ys_sc[i] = ys
            geo_sc[i] = geo
            q_sc[:, c] = q_sc[:, c] + q.reshape(9, 16, 128)
        return 0

    lax.fori_loop(0, groups, front, 0)

    for m in range(9):
        l = 0 if m == 0 else 1 if m < 4 else 2
        m_sc[m] = nn(q_sc[m].reshape(CELLS * 16, 128).astype(BF), c_sc[l]).astype(BF).reshape(CELLS, 16, 128)

    def middle(gi, _):
        ids = [gi * G + i for i in range(G)]
        cells = [list_c[i] for i in ids]
        wout = jnp.concatenate([wout_b[...]] * (L // 128), axis=1)
        mts = [nt(ident, m_sc[:, c].reshape(144, 128)).astype(BF) for c in cells]
        yss = [ys_sc[i] for i in ids]
        ps = [nn(w_mixT[...], sec_sc[i]) + nn(mt, ys) for i, mt, ys in zip(ids, mts, yss)]
        outs = []
        for i, p, ys in zip(ids, ps, yss):
            w = geo_sc[i, 7:8, :]
            mixed, d = silu_both(p)
            eps = jnp.sum(mixed * wout, axis=0, keepdims=True)
            g = (d * wout * w).astype(BF)
            we = eps * w
            hi = we.astype(BF).astype(F32)
            en = nt(jnp.where(iota((16, L), 0) == 0, hi, jnp.where(iota((16, L), 0) == 1, we - hi, 0.0)).astype(BF), ys[0:16])
            outs.append((eps, g, en, nt(ys, g)))
        for i, c, (eps, g, en, dm) in zip(ids, cells, outs):
            g_sc[i] = g
            eps_sc[i] = eps
            dm_sc[:, c] = dm_sc[:, c] + dm.reshape(9, 16, 128)
            en_sc[c] = en_sc[c] + en[0:8]
        return 0

    lax.fori_loop(0, groups, middle, 0)

    for m in range(9):
        l = 0 if m == 0 else 1 if m < 4 else 2
        dq_sc[m] = nt(dm_sc[m].reshape(CELLS * 16, 128).astype(BF), c_sc[l]).astype(BF).reshape(CELLS, 16, 128)

    def back(gi, _):
        ids = [gi * G + i for i in range(G)]
        cells = [list_c[i] for i in ids]
        dqs = [dq_sc[:, c].reshape(144, 128) for c in cells]
        dqts = [nt(ident, v).astype(BF) for v in dqs]
        gs = [g_sc[i] for i in ids]
        secs = [sec_sc[i] for i in ids]
        ts = [nn(v, ys_sc[i]) for i, v in zip(ids, dqts)]
        dpres, dys, dws = [], [], []
        for i, c, g, sb, t, dq in zip(ids, cells, gs, secs, ts, dqs):
            w = geo_sc[i, 7:8, :]
            sf = sb.astype(F32)
            dsec = nn(w_mix[0:128, :], g) + w * t
            dws.append(eps_sc[i] + jnp.sum(sf * t, axis=0, keepdims=True))
            both = jnp.concatenate([g, (sf * w).astype(BF)], axis=0)
            dys.append(nn(jnp.concatenate([m_sc[:, c].reshape(144, 128), dq], axis=1), both))
            dfirst = nn(w_hid[...], (dsec * d2_sc[i].astype(F32)).astype(BF))
            dpres.append((dfirst * d1_sc[i].astype(F32)).astype(BF))
        adds = []
        for i, dpre, dyf, dw in zip(ids, dpres, dys, dws):
            dbasis = nn(w_radrow[48:64, :], dpre)[0:8]
            geo = geo_sc[i]
            rx, ry, rz, live, code, slot, s = [geo[j : j + 1] for j in range(7)]
            d2, inv, dist, nx, ny, nz = sphere(rx, ry, rz)
            m_slot = slot == sub16
            m_s = s == sub16
            dy = [
                jnp.sum(jnp.where(m_s, dyf[16 * m : 16 * m + 16], 0.0), axis=0, keepdims=True) for m in range(1, 9)
            ]
            y1, y2, y3, y4, y5, y6, y7, y8 = dy
            ax = y1 + root_three * (ny * y4 + nz * y7 + nx * y8)
            ay = y2 + root_three * (nx * y4 + nz * y5 - ny * y8)
            az = y3 + root_three * (ny * y5 + nx * y7) + 3.0 * nz * y6
            arg = (dist - (0.5 + 2.0 * iota((8, L), 0, F32))) * 0.5
            basis = jnp.exp(-(arg * arg))
            dd = -jnp.sum(dbasis * basis * arg, axis=0, keepdims=True)
            dd = dd - (ax * nx + ay * ny + az * nz) * inv
            u = jnp.maximum(1.0 - d2 * (1.0 / 144.0), 0.0)
            radial = dd * inv + dw * live * u * (-4.0 / 144.0)
            grads = [a * inv + r * radial for a, r in ((ax, rx), (ay, ry), (az, rz))]
            other = jnp.concatenate([jnp.where(m_slot, -v, 0.0) for v in grads] + [jnp.zeros((16, L), F32)], axis=0)
            mine = jnp.concatenate([jnp.where(m_s, v, 0.0) for v in grads] + [jnp.zeros((16, L), F32)], axis=0)
            where32 = iota((32, L), 0, F32)
            oh = jnp.concatenate([onoff(code == where32), onoff(where32 == 13.0)], axis=1).astype(BF)
            adds.append(nt(oh, jnp.concatenate([other, mine], axis=1).astype(BF)))
        for c, f in zip(cells, adds):
            f_sc[c] = f_sc[c] + f
        return 0

    lax.fori_loop(0, groups, back, 0)

    fa = f_sc[...].reshape(CELLS * 32, 64)
    fh = fa.astype(BF)
    fl = (fa - fh.astype(F32)).astype(BF)
    force_out[...] = jnp.concatenate([nn(fold[...], fh) + nn(fold[...], fl), jnp.zeros((144, 64), F32)], axis=1)
    energy_out[...] = en_sc[:, 0, :] + en_sc[:, 1, :]


def fold_matrix():
    m = np.zeros((144, CELLS * 32), np.float32)
    for c in range(CELLS):
        x, y, z = c // (CY * CZ), c // CZ % CY, c % CZ
        for k in range(27):
            m[((x + k // 9) * 6 + y + k // 3 % 3) * 4 + z + k % 3, c * 32 + k] = 1
    return m


def edge_call(occ_ext, feats, rows, neigh, counts, w_atom, w_rad, w_hid, w_ten, w_mix, w_out):
    V = pltpu.VMEM
    vm = pl.BlockSpec(memory_space=pltpu.VMEM)
    return pl.pallas_call(
        edge_kernel,
        out_shape=(jax.ShapeDtypeStruct((CELLS, 16), F32), jax.ShapeDtypeStruct((144, 128), F32)),
        in_specs=[pl.BlockSpec(memory_space=pltpu.SMEM)] + [vm] * 11,
        out_specs=(vm, vm),
        scratch_shapes=[
            pltpu.SMEM((MAXCH,), jnp.int32),
            pltpu.SMEM((MAXCH,), jnp.int32),
            V((CELLS, 8, 128), jnp.int32),
            V((CELLS, 16, 1024), BF),
            V((CELLS, 64, 128), BF),
            V((CELLS, 64, L), F32),
            V((128, 128), BF),
            V((128, 128), BF),
            V((128, 128), BF),
            V((128, 128), F32),
            V((128, 128), BF),
            V((128, 128), F32),
            V((3, 128, 128), BF),
            V((9, CELLS, 16, 128), F32),
            V((9, CELLS, 16, 128), F32),
            V((9, CELLS, 16, 128), BF),
            V((9, CELLS, 16, 128), BF),
            V((CELLS, 32, 64), F32),
            V((CELLS, 8, 16), F32),
            V((MAXCH, 128, L), BF),
            V((MAXCH, 128, L), BF),
            V((MAXCH, 128, L), BF),
            V((MAXCH, 128, L), BF),
            V((MAXCH, 144, L), BF),
            V((MAXCH, 8, L), F32),
            V((MAXCH, 1, L), F32),
        ],
        compiler_params=pltpu.CompilerParams(vmem_limit_bytes=60 * 1024 * 1024),
        name="edges",
    )(occ_ext, feats, rows, neigh, counts, w_atom, w_rad, w_hid, w_ten, w_mix, w_out, jnp.asarray(fold_matrix(), BF))


def wanted(axis, step):
    return lax.rem(lax.axis_index(axis) + step + lax.axis_size(axis), lax.axis_size(axis))


def meet():
    barrier = pltpu.get_barrier_semaphore()
    for axis in ("gx", "gy", "gz"):
        for step in (-1, 1):
            pl.semaphore_signal(
                barrier, inc=1, device_id={axis: wanted(axis, step)}, device_id_type=pl.DeviceIdType.MESH
            )
    pl.semaphore_wait(barrier, 6)


def sent(src, dst, send, recv, axis, step):
    copy = pltpu.make_async_remote_copy(
        src_ref=src,
        dst_ref=dst,
        send_sem=send,
        recv_sem=recv,
        device_id={axis: wanted(axis, step)},
        device_id_type=pl.DeviceIdType.MESH,
    )
    copy.start()
    return copy


def halo_kernel(pos, occ, feat, feat_ext, rows_ext, send, recv):
    table = jnp.concatenate(
        [pos[0], pos[1], pos[2], occ[...].astype(F32), jnp.zeros((CELLS, 64), F32)], axis=1
    )
    for x in range(CX):
        for y in range(CY):
            for z in range(CZ):
                c = (x * CY + y) * CZ + z
                rows_ext[x + 1, y + 1, z + 1] = table[c : c + 1]
                feat_ext[x + 1, y + 1, z + 1] = feat[c]
    meet()
    inner_y, inner_z = pl.ds(1, CY), pl.ds(1, CZ)
    everything = slice(None)
    places = (
        ("gx", CX, lambda i: (pl.ds(i, 1), inner_y, inner_z)),
        ("gy", CY, lambda i: (everything, pl.ds(i, 1), inner_z)),
        ("gz", CZ, lambda i: (everything, everything, pl.ds(i, 1))),
    )
    for stage, (axis, n, at) in enumerate(places):
        copies = []
        for way, (step, mine, theirs) in enumerate(((-1, 1, n + 1), (1, n, 0))):
            for which, array in enumerate((feat_ext, rows_ext)):
                j = stage * 4 + way * 2 + which
                copies.append(
                    sent(array.at[at(mine)], array.at[at(theirs)], send.at[j], recv.at[j], axis, step)
                )
        for copy in copies:
            copy.wait()


def halo_call(pos, occ, feat):
    vm = pl.BlockSpec(memory_space=pltpu.VMEM)
    return pl.pallas_call(
        halo_kernel,
        out_shape=(
            jax.ShapeDtypeStruct((CX + 2, CY + 2, CZ + 2, 16, 128), BF),
            jax.ShapeDtypeStruct((CX + 2, CY + 2, CZ + 2, 1, 128), F32),
        ),
        in_specs=[vm] * 3,
        out_specs=(vm, vm),
        scratch_shapes=[pltpu.SemaphoreType.DMA((12,)), pltpu.SemaphoreType.DMA((12,))],
        compiler_params=pltpu.CompilerParams(collective_id=0, has_side_effects=True),
        name="halo",
    )(pos, occ, feat)


def fold_kernel(grid, out, acc, got_x, got_y, got_z, send, recv):
    acc[...] = grid[...]
    meet()
    inner_x, inner_y = pl.ds(1, CX), pl.ds(1, CY)
    everything = slice(None)
    places = (
        ("gx", CX, got_x, lambda i: (pl.ds(i, 1), everything, everything)),
        ("gy", CY, got_y, lambda i: (inner_x, pl.ds(i, 1), everything)),
        ("gz", CZ, got_z, lambda i: (inner_x, inner_y, pl.ds(i, 1))),
    )
    for stage, (axis, n, got, at) in enumerate(places):
        copies = []
        for way, (step, rim) in enumerate(((-1, 0), (1, n + 1))):
            j = stage * 2 + way
            copies.append(sent(acc.at[at(rim)], got.at[way], send.at[j], recv.at[j], axis, step))
        for way, edge in enumerate((n, 1)):
            copies[way].wait()
            acc[at(edge)] = acc[at(edge)] + got[way]
    lines = []
    for x in range(CX):
        for y in range(CY):
            for z in range(CZ):
                lines.append(acc[x + 1, y + 1, z + 1])
    lines = jnp.concatenate(lines, axis=0)
    for d in range(3):
        out[d] = lines[:, 16 * d : 16 * d + 16]


def fold_call(grid):
    vm = pl.BlockSpec(memory_space=pltpu.VMEM)
    V = pltpu.VMEM
    return pl.pallas_call(
        fold_kernel,
        out_shape=jax.ShapeDtypeStruct((3, CELLS, 16), F32),
        in_specs=[vm],
        out_specs=vm,
        scratch_shapes=[
            V((CX + 2, CY + 2, CZ + 2, 1, 128), F32),
            V((2, 1, CY + 2, CZ + 2, 1, 128), F32),
            V((2, CX, 1, CZ + 2, 1, 128), F32),
            V((2, CX, CY, 1, 1, 128), F32),
            pltpu.SemaphoreType.DMA((6,)),
            pltpu.SemaphoreType.DMA((6,)),
        ],
        compiler_params=pltpu.CompilerParams(collective_id=1, has_side_effects=True),
        name="fold",
    )(grid)


def on_device(
    positions, occupancy, neighbours, edge_counts, atom_features, w_atom, w_radial, w_hidden, w_tensor, w_mix, w_out
):
    occ = jnp.broadcast_to(occupancy.reshape(CELLS, 1), (CELLS, 16))
    feats, rows = halo_call(positions.reshape(3, CELLS, 16), occ, atom_features.reshape(CELLS, 16, 128))
    rows = rows.reshape(144, 128)
    energy, forces = edge_call(
        rows[:, 48].astype(jnp.int32),
        feats.reshape(144, 16, 128),
        rows,
        neighbours.reshape(CELLS, 16, 64),
        edge_counts.reshape(CELLS, 16),
        w_atom, w_radial, w_hidden, w_tensor, w_mix, w_out.reshape(1, 128),
    )
    forces = fold_call(forces.reshape(CX + 2, CY + 2, CZ + 2, 1, 128))
    return energy.reshape(CX, CY, CZ, 16), forces.reshape(3, CX, CY, CZ, 16)


def solution(mesh):
    cells = P("gx", "gy", "gz", None)
    placed = (
        P(None, "gx", "gy", "gz", None),
        P("gx", "gy", "gz"),
        P("gx", "gy", "gz", None, None),
        cells,
        P("gx", "gy", "gz", None, None),
        P(), P(), P(), P(), P(), P(),
    )
    return jax.shard_map(
        on_device,
        mesh=mesh,
        in_specs=placed,
        out_specs=(cells, P(None, "gx", "gy", "gz", None)),
        check_vma=False,
    )
```

profile of v0, /device:TPU:1, one launch (start us, length us, event | category | flops | bytes accessed | tf_op | source)
XLA Modules:
  0.0 110.9 jit_solution(607254158351759941)
XLA Ops:
  0.6 0.0 copy-start.1
  0.6 0.7 copy-done.1
  1.3 0.1 copy.16
  1.4 0.1 broadcast_in_dim.7
  1.5 0.0 copy-start
  1.5 0.7 broadcast_in_dim.8.occ
  2.2 0.0 copy-done
  2.2 0.7 copy.17.w_ten
  2.9 25.9 %halo.1 = (bf16[6,6,4,16,128]{4,3,2,1,0:T(8,128)(2,1)}, f32[6,6,4,1,128]{4,3,2,1,0:T(1,128)}) custom-call(f32[3,32,16]{2,1,0:T(8,128)} %bitcast.17, s32[32,16]{1,0:T(8,128)} %broadcast_in_dim.8.occ, bf16[32,16,128]{2,1,0:T(8,128)(2,1)} %bitcast.15), custom_call_target="tpu_custom_call" | custom-call | tf_op jit(solution)/shard_map/halo/pallas_call | solution.py:435
  28.9 1.7 %fusion.occ_s = s32[144]{0:T(256)} fusion(f32[144,128]{1,0:T(8,128)} %bitcast.11), kind=kLoop, calls=%fused_computation.1 | loop fusion | flops 144 | bytes 1152 | tf_op jit(solution)/shard_map/convert_element_type | solution.py:505
  30.5 69.2 %edges.1 = (f32[32,16]{1,0:T(8,128)}, f32[144,128]{1,0:T(8,128)}) custom-call(s32[144]{0:T(256)} %fusion.occ_s, bf16[144,16,128]{2,1,0:T(8,128)(2,1)} %bitcast.10, f32[144,128]{1,0:T(8,128)} %bitcast.12, s32[32,16,64]{2,1,0:T(8,128)} %bitcast.13, s32[32,16]{1,0:T(8,128)} %bitcast.18, bf16[128,128]{1,0:T(8,128)(2,1)} %w_atom.1, bf16[8,128]{1,0:T(8,128)(2,1)} %w_rad.1, ...), custom_call_target="tpu_custom_call" | custom-call | tf_op jit(solution)/shard_map/edges/pallas_call | solution.py:338
  99.7 9.7 %fold.2 = f32[3,32,16]{2,1,0:T(8,128)} custom-call(f32[6,6,4,1,128]{4,3,2,1,0:T(1,128)} %bitcast.16), custom_call_target="tpu_custom_call" | custom-call | tf_op jit(solution)/shard_map/fold/pallas_call | solution.py:480
  109.4 1.4 %copy.19 = f32[3,4,4,2,16]{4,3,2,1,0:T(2,128)} copy(f32[3,4,4,2,16]{4,3,2,1,0:T(2,128)} %bitcast.14) | data formatting | bytes 12288
Async XLA Ops:
  0.6 0.7 copy-start.1
  1.5 0.7 copy-start
where the time goes:
time: 111 us
  Pallas kernels  105 us (95%)
  local copies, waits for them, and re-layouts  3.72 us (3%)
  other arithmetic  1.66 us (1%)
    pallas_call x1, Pallas kernels, edge_call(): pl.pallas_call(edge_kernel, out_shape=(jax.ShapeDtypeStruct((CELLS, 16),...  69.2 us
    pallas_call x1, Pallas kernels, halo_call(): pl.pallas_call(halo_kernel, out_shape=(jax.ShapeDtypeStruct((CX + 2, CY +...  25.9 us
    pallas_call x1, Pallas kernels, fold_call(): pl.pallas_call(fold_kernel, out_shape=jax.ShapeDtypeStruct((3, CELLS, 16)...  9.74 us
    unnamed x7, local copies, waits for them, and re-layouts  2.95 us

commit v1 on v0

v1 whole, which is shorter than its diff:
```python
import numpy as np
import jax
import jax.numpy as jnp
from jax import lax
from jax.experimental import pallas as pl
from jax.experimental.pallas import tpu as pltpu
from jax.sharding import PartitionSpec as P

F32 = jnp.float32
BF = jnp.bfloat16
I32 = jnp.int32
root_three = 1.7320508075688772
L = 256
G = 8
CX, CY, CZ = 4, 4, 2
EX, EY, EZ = CX + 2, CY + 2, CZ + 2
CELLS = CX * CY * CZ
GHOSTED = EX * EY * EZ
MAXCH = CELLS * (1024 // L)


def nn(a, b):
    return lax.dot_general(a, b, (((1,), (0,)), ((), ())), preferred_element_type=F32)


def nt(a, b):
    return lax.dot_general(a, b, (((1,), (1,)), ((), ())), preferred_element_type=F32)


def iota(shape, dim, dtype=I32):
    return lax.broadcasted_iota(I32, shape, dim).astype(dtype)


def onoff(mask):
    return jnp.where(mask, 1.0, 0.0).astype(F32)


def eye(n, m):
    return onoff(iota((n, m), 0) == iota((n, m), 1)).astype(BF)


def place_of(c):
    return c // (CY * CZ), c // CZ % CY, c % CZ


def ext_at(x, y, z):
    return (x * EY + y) * EZ + z


def prepare_weights(w_atom, w_rad, w_hid, w_ten_t, w_mix, w_out, mats, radpad, wout_b):
    ident = eye(128, 128)
    half = 0.5
    mats[0] = (half * nt(ident, w_atom[...])).astype(BF)
    mats[1] = (half * nt(ident, w_hid[...])).astype(BF)
    mats[2] = (half * nt(ident, w_mix[0:128, :])).astype(BF)
    rad = jnp.concatenate([jnp.zeros((48, 128), F32), w_rad[...].astype(F32), jnp.zeros((72, 128), F32)], axis=0)
    mats[3] = rad.astype(BF)
    radpad[...] = half * nt(ident, rad.astype(BF))
    wout_b[...] = jnp.sum(
        jnp.where(iota((128, 128), 0) == iota((128, 128), 1), w_out[...], 0.0), axis=1, keepdims=True
    ) * jnp.ones((128, 128), F32)
    tail = w_mix[128:224, :]
    for l in range(3):
        sel = onoff(iota((96, 32), 0) == 3 * iota((96, 32), 1) + l).astype(BF)
        spread = nt(ident, nn(sel, w_ten_t[...]).astype(BF)).astype(BF)
        mats[4 + l] = (0.0625 * nn(spread, tail)).astype(BF)


def prepare_edges(rows, rows2, occ_sp, neigh, counts, rank_out, code_out, rt_out, list_out):
    for x in range(EX):
        for y in range(EY):
            for z in range(EZ):
                at = ext_at(x, y, z)
                rows2[at : at + 1, :] = rows[x, y, z]
    occ_sp[...] = nn(rows2[...].astype(BF), onoff(iota((128, 128), 0) == 48).astype(BF))
    counts_t = nt(eye(16, 16), counts[...].astype(F32).astype(BF))
    lane64 = iota((8, 128), 1)
    low = lane64 < 64
    k_of = jnp.where(low, lane64, lane64 - 64).astype(F32)
    s_of = jnp.where(low, iota((8, 128), 0), iota((8, 128), 0) + 8)
    s_f = s_of.astype(F32)
    masks = []
    for c in range(CELLS):
        x, y, z = place_of(c)
        nb = jnp.concatenate([neigh[c, 0:8, :], neigh[c, 8:16, :]], axis=1)
        code_out[c] = nb
        cnt = jnp.where(low, counts_t[0:8, c : c + 1], counts_t[8:16, c : c + 1])
        code = lax.shift_right_logical(nb, 4)
        slot = lax.bitwise_and(nb, 15).astype(F32)
        occ_n = jnp.zeros((8, 128), F32)
        for k in range(27):
            at = ext_at(x + k // 9, y + k // 3 % 3, z + k % 3)
            occ_n = jnp.where(code == k, occ_sp[at : at + 1, :], occ_n)
        at = ext_at(x + 1, y + 1, z + 1)
        live = (k_of < cnt) & (slot < occ_n) & (s_f < occ_sp[at : at + 1, :]) & (nb != 208 + s_of)
        masks.append(onoff(live))
    mask = jnp.concatenate(masks, axis=0)
    mask_b = mask.astype(BF)
    upto = nn(mask_b, onoff(iota((128, 128), 0) <= iota((128, 128), 1)).astype(BF))
    total = nn(mask_b, jnp.ones((128, 128), BF))
    ri, ci = iota((256, 256), 0), iota((256, 256), 1)
    before = onoff((lax.shift_right_logical(ri, 3) == lax.shift_right_logical(ci, 3)) & (ci < ri)).astype(BF)
    base = nn(before, total.astype(BF))
    rank_out[...] = jnp.where(mask > 0.5, upto - 1.0 + base, -1.0).astype(I32).reshape(CELLS, 8, 128)
    n = (base + total).reshape(CELLS, 8, 128)[:, 7, :].astype(I32)
    chunks = lax.shift_right_logical(n + (L - 1), L.bit_length() - 1).astype(F32)
    ends = nn(onoff(iota((CELLS, CELLS), 1) <= iota((CELLS, CELLS), 0)).astype(BF), chunks.astype(BF))
    t = iota((CELLS, 128), 1, F32)
    done = ends <= t
    cell = jnp.minimum(jnp.sum(onoff(done), axis=0, keepdims=True), CELLS - 1.0)
    start = jnp.max(jnp.where(done, ends, 0.0), axis=0, keepdims=True)
    all_of = ends[CELLS - 1 : CELLS]
    first = jnp.where(t[0:1] < all_of, (t[0:1] - start) * L, 4096.0)
    list_out[...] = jnp.concatenate([cell, first, all_of, jnp.zeros((5, 128), F32)], axis=0).astype(I32)

    lane = iota((32, 128), 1)
    code_i = iota((32, 128), 0)
    ca = code_i // 9
    cb = code_i // 3 - 3 * ca
    cc = code_i - 3 * (code_i // 3)
    coord = lax.shift_right_logical(lane, 4)
    step = jnp.where(coord == 0, ca, jnp.where(coord == 1, cb, jnp.where(coord == 2, cc, 1))) - 1
    shift = 5.0 * step.astype(F32)
    pick = eye(48, 128)
    for c in range(CELLS):
        x, y, z = place_of(c)
        parts = []
        for k in range(0, 27, 3):
            at = ext_at(x + k // 9, y + k // 3 % 3, z)
            parts.append(rows2[at : at + 3, :])
        parts.append(jnp.zeros((5, 128), F32))
        r27 = jnp.concatenate(parts, axis=0) + shift
        hi = r27.astype(BF)
        rest = r27 - hi.astype(F32)
        mid = rest.astype(BF)
        lo = (rest - mid.astype(F32)).astype(BF)
        cat = jnp.concatenate([hi, mid, lo, jnp.zeros((32, 128), BF)], axis=0)
        rt_out[c] = nt(pick, cat).astype(BF)


def silu_both(h):
    t = jnp.tanh(h)
    a = 1.0 + t
    return h * a, a * (1.0 + h * (1.0 - t))


def rows16(v):
    return jnp.broadcast_to(v, (16, v.shape[1])).astype(BF)


def edge_kernel(
    list_s, feats, rank_r, code_r, rt_r, mats, radpad, wout_b, w_mix, w_hid, fold, foldc,
    energy_out, force_out,
    q_sc, dm_sc, m_sc, dq_sc, f_sc, en_sc, sec_sc, d1_sc, d2_sc, g_sc, ys_sc, geo_sc, eps_sc,
):
    groups = lax.div(list_s[2, 0] + (G - 1), G)
    ident = eye(128, 128)
    q_sc[...] = jnp.zeros_like(q_sc)
    dm_sc[...] = jnp.zeros_like(dm_sc)
    f_sc[...] = jnp.zeros_like(f_sc)
    en_sc[...] = jnp.zeros_like(en_sc)
    sub16 = iota((16, L), 0, F32)
    one = jnp.ones((16, L), BF)
    zero = jnp.zeros((16, L), BF)

    def ids_of(gi):
        ids = [gi * G + i for i in range(G)]
        return ids, [list_s[0, i] for i in ids]

    def sphere(rx, ry, rz):
        d2 = rx * rx + ry * ry + rz * rz + 0.01
        inv = lax.rsqrt(d2)
        return d2, inv, d2 * inv, rx * inv, ry * inv, rz * inv

    def front(gi, _):
        ids, cells = ids_of(gi)
        atts, tabs = [], []
        r_of = iota((L, 128), 0, F32).astype(BF)
        s_lane = iota((1, 128), 1)
        sub = iota((16, 128), 0)
        for i, c in zip(ids, cells):
            rk = rank_r[c] - list_s[1, i]
            rk = jnp.where((rk >= 0) & (rk < L), rk, -1).astype(F32)
            nb = code_r[c]
            code_f = lax.shift_right_logical(nb, 4).astype(F32)
            slot_f = lax.bitwise_and(nb, 15).astype(F32)
            ps, att = [], []
            for j in range(8):
                target = jnp.concatenate([jnp.broadcast_to(rk[j : j + 1], (16, 128)).astype(BF)] * (L // 16), axis=0)
                ps.append(jnp.where(r_of == target, jnp.ones((L, 128), BF), jnp.zeros((L, 128), BF)))
                s_row = jnp.where(s_lane < 64, float(j), float(j + 8))
                a = jnp.where(
                    sub == 0, code_f[j : j + 1], jnp.where(sub == 1, slot_f[j : j + 1], jnp.where(sub == 2, s_row, 1.0))
                )
                att.append(a.astype(BF))
            atts.append(nt(jnp.concatenate(att, axis=1), jnp.concatenate(ps, axis=1)))
        for c in cells:
            x = lax.div(c, CY * CZ)
            left = c - x * (CY * CZ)
            y = lax.div(left, CZ)
            z = left - y * CZ
            parts = [
                feats[pl.ds(((x + k // 3) * EY + y + k % 3) * EZ + z, 3)].reshape(48, 128) for k in range(9)
            ]
            parts.append(jnp.zeros((80, 128), BF))
            t = nt(mats[0], jnp.concatenate(parts, axis=0))
            tabs.append(jnp.concatenate([t[:, 0:384], t[:, 384:512] + radpad[...]], axis=1).astype(BF))
        pres, rest = [], []
        for i, c, att, tab in zip(ids, cells, atts, tabs):
            code, slot, s, live = att[0:1], att[1:2], att[2:3], att[3:4]
            oh27 = onoff(code == iota((32, L), 0, F32)).astype(BF)
            m_slot = slot == sub16
            m_s = s == sub16
            rt = rt_r[c]
            got = nn(rt, jnp.concatenate([oh27, oh27, oh27, jnp.zeros((32, L), BF)], axis=0))
            rtf = rt.astype(F32)
            centre = rtf[:, 13:14] + (rtf[:, 45:46] + rtf[:, 77:78])
            rel = []
            for d in range(3):
                sl = slice(16 * d, 16 * d + 16)
                rel.append(
                    jnp.sum(jnp.where(m_slot, got[sl], 0.0) - jnp.where(m_s, centre[sl], 0.0), axis=0, keepdims=True)
                )
            rx, ry, rz = rel
            d2, inv, dist, nx, ny, nz = sphere(rx, ry, rz)
            u = jnp.maximum(1.0 - d2 * (1.0 / 144.0), 0.0)
            w = live * (u * u)
            arg = (dist - (0.5 + 2.0 * iota((8, L), 0, F32))) * 0.5
            basis = jnp.exp(-(arg * arg))
            slot01 = onoff(m_slot).astype(BF)
            s01 = onoff(m_s).astype(BF)
            code16 = rows16(code)
            tiles = [jnp.where(code16 == float(k), slot01, zero) for k in range(27)]
            tiles[13] = tiles[13] + s01
            tiles.append(jnp.concatenate([basis, jnp.zeros((8, L), F32)], axis=0).astype(BF))
            pres.append(nn(tab, jnp.concatenate(tiles + [zero] * 4, axis=0)))
            ylist = [
                nx, ny, nz, root_three * nx * ny, root_three * ny * nz,
                0.5 * (3.0 * nz * nz - 1.0), root_three * nx * nz, (0.5 * root_three) * (nx * nx - ny * ny),
            ]
            ys = jnp.concatenate([s01] + [s01 * rows16(v) for v in ylist], axis=0)
            geo = jnp.concatenate([rx, ry, rz, live, code, slot, s, w], axis=0)
            rest.append((ys, geo, rows16(w)))
        firsts = [silu_both(v) for v in pres]
        secs = [silu_both(nn(mats[1], f.astype(BF))) for f, _ in firsts]
        qs = []
        for (sec, d), (ys, geo, w16) in zip(secs, rest):
            sb = sec.astype(BF)
            qs.append((sb, nt(ys * jnp.concatenate([w16] * 9, axis=0), sb)))
        for i, c, (f, d1), (sec, d2), (ys, geo, w16), (sb, q) in zip(ids, cells, firsts, secs, rest, qs):
            sec_sc[i] = sb
            d1_sc[i] = d1.astype(BF)
            d2_sc[i] = d2.astype(BF)
            ys_sc[i] = ys
            geo_sc[i] = geo
            q_sc[:, c] = q_sc[:, c] + q.reshape(9, 16, 128)
        return 0

    lax.fori_loop(0, groups, front, 0)

    for m in range(9):
        l = 0 if m == 0 else 1 if m < 4 else 2
        m_sc[m] = nn(q_sc[m].reshape(CELLS * 16, 128).astype(BF), mats[4 + l]).astype(BF).reshape(CELLS, 16, 128)

    def middle(gi, _):
        ids, cells = ids_of(gi)
        wout = jnp.concatenate([wout_b[...]] * (L // 128), axis=1)
        wout_h = 0.5 * wout
        mts = [nt(ident, m_sc[:, c].reshape(144, 128)).astype(BF) for c in cells]
        yss = [ys_sc[i] for i in ids]
        ps = [nn(mats[2], sec_sc[i]) + nn(mt, ys) for i, mt, ys in zip(ids, mts, yss)]
        outs = []
        for i, p, ys in zip(ids, ps, yss):
            w = geo_sc[i, 7:8, :]
            mixed, d = silu_both(p)
            eps = jnp.sum(mixed * wout, axis=0, keepdims=True)
            g = (d * wout_h).astype(BF)
            we = eps * w
            hi = we.astype(BF).astype(F32)
            en = nt(jnp.where(iota((16, L), 0) == 0, hi, jnp.where(iota((16, L), 0) == 1, we - hi, 0.0)).astype(BF), ys[0:16])
            outs.append((eps, g, en, nt(ys * jnp.concatenate([rows16(w)] * 9, axis=0), g)))
        for i, c, (eps, g, en, dm) in zip(ids, cells, outs):
            g_sc[i] = g
            eps_sc[i] = eps
            dm_sc[:, c] = dm_sc[:, c] + dm.reshape(9, 16, 128)
            en_sc[c] = en_sc[c] + en[0:8]
        return 0

    lax.fori_loop(0, groups, middle, 0)

    for m in range(9):
        l = 0 if m == 0 else 1 if m < 4 else 2
        dq_sc[m] = nt(dm_sc[m].reshape(CELLS * 16, 128).astype(BF), mats[4 + l]).astype(BF).reshape(CELLS, 16, 128)

    def back(gi, _):
        ids, cells = ids_of(gi)
        dqs = [dq_sc[:, c].reshape(144, 128) for c in cells]
        dqts = [nt(ident, v).astype(BF) for v in dqs]
        secs = [sec_sc[i] for i in ids]
        ts = [nn(v, ys_sc[i]) for i, v in zip(ids, dqts)]
        dpres, dys, dws = [], [], []
        top = jnp.concatenate([w_mix[0:128, :], jnp.zeros((128, 128), BF)], axis=1)
        for i, c, sb, t, dq in zip(ids, cells, secs, ts, dqs):
            t2 = t + t
            low = jnp.concatenate([m_sc[:, c].reshape(144, 128), dq], axis=1)
            both = nn(jnp.concatenate([top, low], axis=0), jnp.concatenate([g_sc[i], sb], axis=0))
            dsec = both[0:128] + t2
            dws.append(eps_sc[i] + jnp.sum(sb.astype(F32) * t2, axis=0, keepdims=True))
            dys.append(both[128:272])
            dfirst = nn(w_hid[...], (dsec * d2_sc[i].astype(F32)).astype(BF))
            dpres.append((dfirst * d1_sc[i].astype(F32)).astype(BF))
        adds = []
        for i, dpre, dyf, dw in zip(ids, dpres, dys, dws):
            dbasis = nn(mats[3, 48:64, :], dpre)[0:8]
            geo = geo_sc[i]
            rx, ry, rz, live, code, slot, s, w = [geo[j : j + 1] for j in range(8)]
            d2, inv, dist, nx, ny, nz = sphere(rx, ry, rz)
            m_slot = slot == sub16
            m_s = s == sub16
            w2 = w + w
            dy = [
                jnp.sum(jnp.where(m_s, dyf[16 * m : 16 * m + 16], 0.0), axis=0, keepdims=True) * w2 for m in range(1, 9)
            ]
            y1, y2, y3, y4, y5, y6, y7, y8 = dy
            ax = y1 + root_three * (ny * y4 + nz * y7 + nx * y8)
            ay = y2 + root_three * (nx * y4 + nz * y5 - ny * y8)
            az = y3 + root_three * (ny * y5 + nx * y7) + 3.0 * nz * y6
            arg = (dist - (0.5 + 2.0 * iota((8, L), 0, F32))) * 0.5
            basis = jnp.exp(-(arg * arg))
            dd = jnp.sum(dbasis * basis * arg, axis=0, keepdims=True) * (-0.25 * w)
            dd = dd - (ax * nx + ay * ny + az * nz) * inv
            u = jnp.maximum(1.0 - d2 * (1.0 / 144.0), 0.0)
            radial = dd * inv + dw * live * u * (-4.0 / 144.0)
            grads = [a * inv + r * radial for a, r in ((ax, rx), (ay, ry), (az, rz))]
            slot01 = onoff(m_slot).astype(BF)
            s01 = onoff(m_s).astype(BF)
            g16 = [rows16(v) for v in grads]
            parts = [slot01 * -v for v in g16] + [zero] + [s01 * v for v in g16] + [zero]
            where32 = iota((32, L), 0, F32)
            oh = onoff((code == where32) | (where32 == 27.0)).astype(BF)
            adds.append(nt(oh, jnp.concatenate(parts, axis=0)))
        for c, f in zip(cells, adds):
            f_sc[c] = f_sc[c] + f
        return 0

    lax.fori_loop(0, groups, back, 0)

    fa = f_sc[...].reshape(CELLS * 32, 128)
    fh = fa.astype(BF)
    fl = (fa - fh.astype(F32)).astype(BF)
    others = nn(fold[...], fh) + nn(fold[...], fl)
    own = nn(foldc[...], fh) + nn(foldc[...], fl)
    force_out[...] = others + jnp.concatenate([own[:, 64:128], jnp.zeros((GHOSTED, 64), F32)], axis=1)
    energy_out[...] = en_sc[:, 0, :] + en_sc[:, 1, :]


def fold_matrices():
    m = np.zeros((2, GHOSTED, CELLS * 32), np.float32)
    for c in range(CELLS):
        x, y, z = place_of(c)
        for k in range(27):
            m[0, ext_at(x + k // 9, y + k // 3 % 3, z + k % 3), c * 32 + k] = 1
        m[1, ext_at(x + 1, y + 1, z + 1), c * 32 + 27] = 1
    return m


PREPARED = (
    jax.ShapeDtypeStruct((CELLS, 8, 128), I32),
    jax.ShapeDtypeStruct((CELLS, 8, 128), I32),
    jax.ShapeDtypeStruct((CELLS, 48, 128), BF),
    jax.ShapeDtypeStruct((8, 128), I32),
    jax.ShapeDtypeStruct((7, 128, 128), BF),
    jax.ShapeDtypeStruct((128, 128), F32),
    jax.ShapeDtypeStruct((128, 128), F32),
)


def edge_stage(feats, prepared, w_mix, w_hid):
    rank, code, rt, todo, mats, radpad, wout_b = prepared
    V = pltpu.VMEM
    vm = pl.BlockSpec(memory_space=pltpu.VMEM)
    folds = fold_matrices()
    return pl.pallas_call(
        edge_kernel,
        out_shape=(jax.ShapeDtypeStruct((CELLS, 16), F32), jax.ShapeDtypeStruct((GHOSTED, 128), F32)),
        in_specs=[pl.BlockSpec(memory_space=pltpu.SMEM)] + [vm] * 11,
        out_specs=(vm, vm),
        scratch_shapes=[
            V((9, CELLS, 16, 128), F32),
            V((9, CELLS, 16, 128), F32),
            V((9, CELLS, 16, 128), BF),
            V((9, CELLS, 16, 128), BF),
            V((CELLS, 32, 128), F32),
            V((CELLS, 8, 16), F32),
            V((MAXCH, 128, L), BF),
            V((MAXCH, 128, L), BF),
            V((MAXCH, 128, L), BF),
            V((MAXCH, 128, L), BF),
            V((MAXCH, 144, L), BF),
            V((MAXCH, 8, L), F32),
            V((MAXCH, 1, L), F32),
        ],
        compiler_params=pltpu.CompilerParams(vmem_limit_bytes=60 * 1024 * 1024),
        name="edges",
    )(todo, feats, rank, code, rt, mats, radpad, wout_b, w_mix, w_hid, jnp.asarray(folds[0], BF), jnp.asarray(folds[1], BF))


MESH = pl.DeviceIdType.MESH
AROUND = tuple((dx, dy) for dx in (-1, 0, 1) for dy in (-1, 0, 1) if (dx, dy) != (0, 0))


def peer(dx, dy, dz):
    there = {}
    for axis, step in (("gx", dx), ("gy", dy), ("gz", dz)):
        size = lax.axis_size(axis)
        there[axis] = lax.rem(lax.axis_index(axis) + (step + size), size)
    return there


def greet():
    barrier = pltpu.get_barrier_semaphore()
    for dx, dy, dz in [(0, 0, -1), (0, 0, 1)] + [(dx, dy, 0) for dx, dy in AROUND]:
        pl.semaphore_signal(barrier, inc=1, device_id=peer(dx, dy, dz), device_id_type=MESH)
    return barrier


def sent(src, dst, send, recv, there):
    copy = pltpu.make_async_remote_copy(
        src_ref=src, dst_ref=dst, send_sem=send, recv_sem=recv, device_id=there, device_id_type=MESH
    )
    copy.start()
    return copy


def border(step, n):
    return pl.ds(1, n) if step == 0 else pl.ds(1 if step < 0 else n, 1)


def ghost(step, n):
    return pl.ds(1, n) if step == 0 else pl.ds(n + 1 if step < 0 else 0, 1)


def halo_kernel(
    occ_s, pos, feat, neigh, counts, w_atom, w_rad, w_hid, w_ten_t, w_mix, w_out,
    feat_ext, rank, code, rt, todo, mats, radpad, wout_b,
    rows, rows2, occ_sp, send, recv,
):
    barrier = greet()
    table = jnp.concatenate([pos[0], pos[1], pos[2], jnp.zeros((CELLS, 80), F32)], axis=1)
    lane = iota((1, 128), 1)
    for c in range(CELLS):
        x, y, z = place_of(c)
        rows[x + 1, y + 1, z + 1] = jnp.where(lane < 48, table[c : c + 1], occ_s[x, z, y].astype(F32))
        feat_ext[x + 1, y + 1, z + 1] = feat[c]
    pl.semaphore_wait(barrier, 10)

    def along_z(array, base):
        copies = []
        for j, step in enumerate((-1, 1)):
            at = (pl.ds(1, CX), pl.ds(1, CY))
            src = array.at[at + (border(step, CZ),)]
            dst = array.at[at + (ghost(step, CZ),)]
            copies.append(sent(src, dst, send.at[base + j], recv.at[base + j], peer(0, 0, step)))
        return copies

    def around(array, base):
        copies = []
        for j, (dx, dy) in enumerate(AROUND):
            src = array.at[border(dx, CX), border(dy, CY)]
            dst = array.at[ghost(dx, CX), ghost(dy, CY)]
            copies.append(sent(src, dst, send.at[base + j], recv.at[base + j], peer(dx, dy, 0)))
        return copies

    rows_z = along_z(rows, 0)
    feat_z = along_z(feat_ext, 2)
    for copy in rows_z:
        copy.wait()
    rows_xy = around(rows, 4)
    for copy in feat_z:
        copy.wait()
    feat_xy = around(feat_ext, 12)
    prepare_weights(w_atom, w_rad, w_hid, w_ten_t, w_mix, w_out, mats, radpad, wout_b)
    for copy in rows_xy:
        copy.wait()
    prepare_edges(rows, rows2, occ_sp, neigh, counts, rank, code, rt, todo)
    for copy in feat_xy:
        copy.wait()


def halo_stage(occ, pos, feat, neigh, counts, w_atom, w_rad, w_hid, w_ten_t, w_mix, w_out):
    vm = pl.BlockSpec(memory_space=pltpu.VMEM)
    V = pltpu.VMEM
    out = pl.pallas_call(
        halo_kernel,
        out_shape=(jax.ShapeDtypeStruct((EX, EY, EZ, 16, 128), BF),) + PREPARED,
        in_specs=[pl.BlockSpec(memory_space=pltpu.SMEM)] + [vm] * 10,
        out_specs=(vm,) * 8,
        scratch_shapes=[
            V((EX, EY, EZ, 1, 128), F32),
            V((GHOSTED, 128), F32),
            V((GHOSTED, 128), F32),
            pltpu.SemaphoreType.DMA((20,)),
            pltpu.SemaphoreType.DMA((20,)),
        ],
        compiler_params=pltpu.CompilerParams(
            collective_id=0, has_side_effects=True, vmem_limit_bytes=32 * 1024 * 1024
        ),
        name="halo",
    )(occ, pos, feat, neigh, counts, w_atom, w_rad, w_hid, w_ten_t, w_mix, w_out)
    return out[0], out[1:]


def fold_kernel(grid, out, acc, got_x, got_y, got_xy, got_z, send, recv):
    barrier = greet()
    acc[...] = grid[...]
    pl.semaphore_wait(barrier, 10)
    copies = []
    for j, (dx, dy) in enumerate(AROUND):
        if dx and dy:
            got = got_xy.at[(dx + 1) + (dy + 1) // 2]
        elif dx:
            got = got_x.at[(dx + 1) // 2]
        else:
            got = got_y.at[(dy + 1) // 2]
        rim = (
            pl.ds(1, CX) if dx == 0 else pl.ds(0 if dx < 0 else CX + 1, 1),
            pl.ds(1, CY) if dy == 0 else pl.ds(0 if dy < 0 else CY + 1, 1),
        )
        copies.append((sent(acc.at[rim], got, send.at[j], recv.at[j], peer(dx, dy, 0)), got, dx, dy))
    for copy, got, dx, dy in copies:
        copy.wait()
        at = (border(-dx, CX), border(-dy, CY))
        acc[at] = acc[at] + got[...]
    inner = (pl.ds(1, CX), pl.ds(1, CY))
    copies = []
    for j, (step, rim) in enumerate(((-1, 0), (1, CZ + 1))):
        copies.append(
            sent(acc.at[inner + (pl.ds(rim, 1),)], got_z.at[j], send.at[8 + j], recv.at[8 + j], peer(0, 0, step))
        )
    for j, step in enumerate((-1, 1)):
        copies[j].wait()
        at = inner + (border(-step, CZ),)
        acc[at] = acc[at] + got_z[j]
    lines = []
    for c in range(CELLS):
        x, y, z = place_of(c)
        lines.append(acc[x + 1, y + 1, z + 1])
    lines = jnp.concatenate(lines, axis=0)
    for d in range(3):
        out[d] = lines[:, 16 * d : 16 * d + 16]


def fold_stage(grid):
    vm = pl.BlockSpec(memory_space=pltpu.VMEM)
    V = pltpu.VMEM
    return pl.pallas_call(
        fold_kernel,
        out_shape=jax.ShapeDtypeStruct((3, CELLS, 16), F32),
        in_specs=[vm],
        out_specs=vm,
        scratch_shapes=[
            V((EX, EY, EZ, 1, 128), F32),
            V((2, 1, CY, EZ, 1, 128), F32),
            V((2, CX, 1, EZ, 1, 128), F32),
            V((4, 1, 1, EZ, 1, 128), F32),
            V((2, CX, CY, 1, 1, 128), F32),
            pltpu.SemaphoreType.DMA((10,)),
            pltpu.SemaphoreType.DMA((10,)),
        ],
        compiler_params=pltpu.CompilerParams(collective_id=1, has_side_effects=True),
        name="fold",
    )(grid)


def on_device(
    positions, occupancy, neighbours, edge_counts, atom_features, w_atom, w_radial, w_hidden, w_tensor, w_mix, w_out
):
    feats, prepared = halo_stage(
        occupancy.transpose(0, 2, 1),
        positions.reshape(3, CELLS, 16),
        atom_features.reshape(CELLS, 16, 128),
        neighbours.reshape(CELLS, 16, 64),
        edge_counts.reshape(CELLS, 16),
        w_atom, w_radial, w_hidden, w_tensor.T, w_mix, w_out.reshape(1, 128),
    )
    energy, forces = edge_stage(feats.reshape(GHOSTED, 16, 128), prepared, w_mix, w_hidden)
    forces = fold_stage(forces.reshape(EX, EY, EZ, 1, 128))
    return energy.reshape(CX, CY, CZ, 16), forces.reshape(3, CX, CY, CZ, 16)


def solution(mesh):
    cells = P("gx", "gy", "gz", None)
    placed = (
        P(None, "gx", "gy", "gz", None),
        P("gx", "gy", "gz"),
        P("gx", "gy", "gz", None, None),
        cells,
        P("gx", "gy", "gz", None, None),
        P(), P(), P(), P(), P(), P(),
    )
    return jax.shard_map(
        on_device,
        mesh=mesh,
        in_specs=placed,
        out_specs=(cells, P(None, "gx", "gy", "gz", None)),
        check_vma=False,
    )
```

time: 111 us -> 93.3 us (0.84)
  Pallas kernels: 105 us -> 78.1 us
  local copies, waits for them, and re-layouts: 3.72 us -> 13.9 us
  other arithmetic: 1.66 us -> 0 us
    pallas_call x3, Pallas kernels: 105 us -> 78.1 us  [the longest x1 39.6 us: edge_stage(): pl.pallas_call(edge_kernel, out_shape=(jax.ShapeDtypeStruct((CELLS, 16),...]
    unnamed x7 -> x39, local copies, waits for them, and re-layouts: 2.95 us -> 13.9 us
    convert_element_type x1 -> x0, other arithmetic: 1.66 us -> none  [on_device(): rows[:, 48].astype(jnp.int32)]
where the time goes in v1:
time: 93.3 us; the launch traced here: 92.7 us
  Pallas kernels  78.1 us (84%)
  local copies, waits for them, and re-layouts  13.9 us (15%)
    pallas_call x1, Pallas kernels, edge_stage(): pl.pallas_call(edge_kernel, out_shape=(jax.ShapeDtypeStruct((CELLS, 16),...  39.6 us
    pallas_call x1, Pallas kernels, halo_stage(): pl.pallas_call(halo_kernel, out_shape=(jax.ShapeDtypeStruct((EX, EY, EZ,...  22.3 us
    pallas_call x1, Pallas kernels, fold_stage(): pl.pallas_call(fold_kernel, out_shape=jax.ShapeDtypeStruct((3, CELLS, 16)...  16.2 us
    unnamed x39, local copies, waits for them, and re-layouts  13.9 us

profile of v1, /device:TPU:1, one launch (start us, length us, event | category | flops | bytes accessed | tf_op | source)
XLA Modules:
  0.0 92.7 jit_solution(609614061021486816)
XLA Ops:
  0.6 0.0 copy-start.14
  0.6 0.0 copy-start.15
  0.7 0.0 copy-start.18
  0.7 0.7 copy-done.14
  1.3 0.0 copy-done.15
  1.3 0.0 copy-done.18
  1.3 0.0 copy-start.2
  1.3 0.9 %copy-done.2 = s32[4,4,2,16,64]{4,3,2,1,0:T(8,128)S(1)} copy-done((s32[4,4,2,16,64]{4,3,2,1,0:T(8,128)S(1)}, s32[4,4,2,16,64]{4,3,2,1,0:T(8,128)}, u32[]{:S(2)}) %copy-start.2) | copy-done | bytes 131096
  2.3 0.0 copy-start.4
  2.3 0.8 copy-done.4
  3.1 0.0 copy-start.5
  3.1 0.8 copy-done.5
  3.9 0.0 copy-start.8
  3.9 0.9 copy-done.8
  4.8 0.0 copy-start.11
  4.8 0.8 copy-done.11
  5.6 0.0 copy-start.12
  5.6 0.8 copy-done.12
  6.3 0.0 copy-start.13
  6.3 0.7 copy-done.13
  7.0 0.0 copy-start.17
  7.1 0.7 copy-done.17
  7.7 22.3 %halo.1 = (bf16[6,6,4,16,128]{4,3,2,1,0:T(8,128)(2,1)S(1)}, s32[32,8,128]{2,1,0:T(8,128)S(1)}, s32[32,8,128]{2,1,0:T(8,128)S(1)}, bf16[32,48,128]{2,1,0:T(8,128)...) custom-call(s32[4,2,4]{2,1,0:T(2,128)S(1)} %bitcast.17, ...), custom_call_target="tpu_custom_call" | custom-call | tf_op jit(solution)/shard_map/halo/pallas_call | solution.py:493
  30.0 0.0 copy-start
  30.0 0.8 copy-done
  30.8 0.0 copy-start.1
  30.8 0.8 copy-done.1
  31.6 0.0 copy-start.3
  31.6 0.7 copy-done.3
  32.3 0.0 copy-start.6
  32.3 0.6 copy-done.6
  33.0 0.0 copy-start.7
  33.0 0.7 copy-done.7
  33.6 0.0 copy-start.9
  33.6 0.6 copy-done.9
  34.2 0.0 copy-start.10
  34.2 0.6 copy-done.10
  34.9 0.0 copy-start.16
  34.9 0.6 copy-done.16
  35.5 39.6 %edges.1 = (f32[32,16]{1,0:T(8,128)}, f32[144,128]{1,0:T(8,128)}) custom-call(s32[8,128]{1,0:T(8,128)} %copy-done.16, bf16[144,16,128]{2,1,0:T(8,128)(2,1)} %bitcast.11, s32[32,8,128]{2,1,0:T(8,128)} %copy-done.6, s32[32,8,128]{2,1,0:T(8,128)} %copy-done.7, bf16[32,48,128]{2,1,0:T(8,128)(2,1)} %copy-done.1, bf16[7,128,128]{2,1,0:T(8,128)(2,1)} %copy-done.3, ...), custom_call_target="tpu_custom_call" | custom-call | tf_op jit(solution)/shard_map/edges/pallas_call | solution.py:383
  75.1 16.2 %fold.2 = f32[3,32,16]{2,1,0:T(8,128)} custom-call(f32[6,6,4,1,128]{4,3,2,1,0:T(1,128)} %bitcast.20), custom_call_target="tpu_custom_call" | custom-call | tf_op jit(solution)/shard_map/fold/pallas_call | solution.py:556
  91.3 1.4 %copy.16 = f32[3,4,4,2,16]{4,3,2,1,0:T(2,128)} copy(f32[3,4,4,2,16]{4,3,2,1,0:T(2,128)} %bitcast.19) | data formatting | bytes 12288
Async XLA Ops:
  0.6 0.7 copy-start.14
  0.6 0.7 copy-start.15
  0.7 0.7 copy-start.18
  1.3 1.0 %copy-start.2 = (s32[4,4,2,16,64]{4,3,2,1,0:T(8,128)S(1)}, s32[4,4,2,16,64]{4,3,2,1,0:T(8,128)}, u32[]{:S(2)}) copy-start(s32[4,4,2,16,64]{4,3,2,1,0:T(8,128)} %param.15) | copy-start | bytes 393220
  2.3 0.8 copy-start.4
  3.1 0.8 copy-start.5
  3.9 0.9 copy-start.8
  4.8 0.8 copy-start.11
  5.6 0.8 copy-start.12
  6.3 0.7 copy-start.13
  7.0 0.7 copy-start.17
  30.0 0.8 copy-start
  30.8 0.8 copy-start.1
  31.6 0.7 copy-start.3
  32.3 0.7 copy-start.6
  33.0 0.7 copy-start.7
  33.6 0.6 copy-start.9
  34.2 0.6 copy-start.10
  34.9 0.6 copy-start.16

commit v2 on v1

--- a/solution.py
+++ b/solution.py
@@ -27,6 +27,10 @@
     return lax.dot_general(a, b, (((1,), (1,)), ((), ())), preferred_element_type=F32)
 
 
+def tn(a, b):
+    return lax.dot_general(a, b, (((0,), (0,)), ((), ())), preferred_element_type=F32)
+
+
 def iota(shape, dim, dtype=I32):
     return lax.broadcasted_iota(I32, shape, dim).astype(dtype)
 
@@ -47,15 +51,15 @@
     return (x * EY + y) * EZ + z
 
 
-def prepare_weights(w_atom, w_rad, w_hid, w_ten_t, w_mix, w_out, mats, radpad, wout_b):
+def prepare_weights(w_atom, w_rad, w_hid, w_ten_t, w_mix, w_out, mats, wout_r, wout_b):
     ident = eye(128, 128)
     half = 0.5
-    mats[0] = (half * nt(ident, w_atom[...])).astype(BF)
+    mats[0] = (half * w_atom[...].astype(F32)).astype(BF)
     mats[1] = (half * nt(ident, w_hid[...])).astype(BF)
     mats[2] = (half * nt(ident, w_mix[0:128, :])).astype(BF)
     rad = jnp.concatenate([jnp.zeros((48, 128), F32), w_rad[...].astype(F32), jnp.zeros((72, 128), F32)], axis=0)
-    mats[3] = rad.astype(BF)
-    radpad[...] = half * nt(ident, rad.astype(BF))
+    mats[3] = (half * rad).astype(BF)
+    wout_r[...] = w_out[...] * jnp.ones((8, 128), F32)
     wout_b[...] = jnp.sum(
         jnp.where(iota((128, 128), 0) == iota((128, 128), 1), w_out[...], 0.0), axis=1, keepdims=True
     ) * jnp.ones((128, 128), F32)
@@ -141,17 +145,31 @@
 def silu_both(h):
     t = jnp.tanh(h)
     a = 1.0 + t
-    return h * a, a * (1.0 + h * (1.0 - t))
+    y = h * a
+    return y, a + y * (1.0 - t)
+
+
+def wide16(v):
+    return jnp.broadcast_to(v, (16, 128)).astype(BF)
 
 
 def rows16(v):
     return jnp.broadcast_to(v, (16, v.shape[1])).astype(BF)
 
 
+def weave(tasks):
+    active = list(tasks)
+    while active:
+        active = [task for task in active if next(task, None) is not None]
+
+
+RX, RY, RZ, LIVE, CODE, SLOT, WHO, WEIGHT, EPS = range(9)
+
+
 def edge_kernel(
-    list_s, feats, rank_r, code_r, rt_r, mats, radpad, wout_b, w_mix, w_hid, fold, foldc,
+    list_s, feats, rank_r, code_r, rt_r, mats, wout_r, wout_b, w_mix, w_hid, fold, foldc,
     energy_out, force_out,
-    q_sc, dm_sc, m_sc, dq_sc, f_sc, en_sc, sec_sc, d1_sc, d2_sc, g_sc, ys_sc, geo_sc, eps_sc,
+    proj_sc, q_sc, dm_sc, m_sc, dq_sc, f_sc, en_sc, sec_sc, d1_sc, d2_sc, g_sc, ys_sc, geo_sc, y_sc, red_sc, gr_sc,
 ):
     groups = lax.div(list_s[2, 0] + (G - 1), G)
     ident = eye(128, 128)
@@ -160,100 +178,122 @@
     f_sc[...] = jnp.zeros_like(f_sc)
     en_sc[...] = jnp.zeros_like(en_sc)
     sub16 = iota((16, L), 0, F32)
-    one = jnp.ones((16, L), BF)
+    proj_sc[...] = nn(feats[...].reshape(GHOSTED * 16, 128), mats[0]).astype(BF).reshape(GHOSTED, 16, 128)
     zero = jnp.zeros((16, L), BF)
+    centres = 0.5 + 2.0 * iota((8, L), 0, F32)
 
     def ids_of(gi):
         ids = [gi * G + i for i in range(G)]
         return ids, [list_s[0, i] for i in ids]
 
-    def sphere(rx, ry, rz):
+    def sphere(gi):
+        rx, ry, rz = geo_sc[gi, RX], geo_sc[gi, RY], geo_sc[gi, RZ]
         d2 = rx * rx + ry * ry + rz * rz + 0.01
         inv = lax.rsqrt(d2)
-        return d2, inv, d2 * inv, rx * inv, ry * inv, rz * inv
+        return rx, ry, rz, d2, inv, d2 * inv, rx * inv, ry * inv, rz * inv
 
     def front(gi, _):
         ids, cells = ids_of(gi)
-        atts, tabs = [], []
-        r_of = iota((L, 128), 0, F32).astype(BF)
+        sixteen = iota((16, 128), 0, F32).astype(BF)
+        lane_l = iota((16, L), 1)
+        unfold = onoff(lax.bitwise_and(lane_l, 15) == iota((16, L), 0)).astype(BF)
+        in_high = lax.shift_right_logical(lane_l, 4) == iota((16, L), 0)
         s_lane = iota((1, 128), 1)
-        sub = iota((16, 128), 0)
-        for i, c in zip(ids, cells):
+        ones = jnp.ones((16, 128), BF)
+        zeros = jnp.zeros((16, 128), BF)
+
+        def find(j, i, c):
             rk = rank_r[c] - list_s[1, i]
-            rk = jnp.where((rk >= 0) & (rk < L), rk, -1).astype(F32)
+            inside = (rk >= 0) & (rk < L)
+            high = jnp.where(inside, lax.shift_right_logical(rk, 4), -1).astype(F32)
+            deep = lax.bitwise_and(rk, 15).astype(F32)
             nb = code_r[c]
             code_f = lax.shift_right_logical(nb, 4).astype(F32)
             slot_f = lax.bitwise_and(nb, 15).astype(F32)
-            ps, att = [], []
-            for j in range(8):
-                target = jnp.concatenate([jnp.broadcast_to(rk[j : j + 1], (16, 128)).astype(BF)] * (L // 16), axis=0)
-                ps.append(jnp.where(r_of == target, jnp.ones((L, 128), BF), jnp.zeros((L, 128), BF)))
-                s_row = jnp.where(s_lane < 64, float(j), float(j + 8))
-                a = jnp.where(
-                    sub == 0, code_f[j : j + 1], jnp.where(sub == 1, slot_f[j : j + 1], jnp.where(sub == 2, s_row, 1.0))
+            left, right = [], []
+            for k in range(8):
+                s_row = jnp.where(s_lane < 64, float(k), float(k + 8))
+                at_high = jnp.where(sixteen == wide16(high[k : k + 1]), ones, zeros)
+                left.append(
+                    jnp.concatenate(
+                        [at_high * wide16(v) for v in (code_f[k : k + 1], slot_f[k : k + 1], s_row)] + [at_high], axis=0
+                    )
                 )
-                att.append(a.astype(BF))
-            atts.append(nt(jnp.concatenate(att, axis=1), jnp.concatenate(ps, axis=1)))
-        for c in cells:
-            x = lax.div(c, CY * CZ)
-            left = c - x * (CY * CZ)
-            y = lax.div(left, CZ)
-            z = left - y * CZ
-            parts = [
-                feats[pl.ds(((x + k // 3) * EY + y + k % 3) * EZ + z, 3)].reshape(48, 128) for k in range(9)
+                right.append(jnp.where(sixteen == wide16(deep[k : k + 1]), ones, zeros))
+            packed = nt(jnp.concatenate(left, axis=1), jnp.concatenate(right, axis=1))
+            yield 1
+            spread = nn(packed.astype(BF), unfold)
+            yield 1
+            code, slot, s, live = [
+                jnp.sum(jnp.where(in_high, spread[16 * a : 16 * a + 16], 0.0), axis=0, keepdims=True) for a in range(4)
             ]
-            parts.append(jnp.zeros((80, 128), BF))
-            t = nt(mats[0], jnp.concatenate(parts, axis=0))
-            tabs.append(jnp.concatenate([t[:, 0:384], t[:, 384:512] + radpad[...]], axis=1).astype(BF))
-        pres, rest = [], []
-        for i, c, att, tab in zip(ids, cells, atts, tabs):
-            code, slot, s, live = att[0:1], att[1:2], att[2:3], att[3:4]
             oh27 = onoff(code == iota((32, L), 0, F32)).astype(BF)
+            rt = rt_r[c]
+            got = nn(rt, jnp.concatenate([oh27, oh27, oh27, jnp.zeros((32, L), BF)], axis=0))
+            for q, v in ((LIVE, live), (CODE, code), (SLOT, slot), (WHO, s)):
+                geo_sc[gi, q, j : j + 1, :] = v
+            yield 1
             m_slot = slot == sub16
             m_s = s == sub16
-            rt = rt_r[c]
-            got = nn(rt, jnp.concatenate([oh27, oh27, oh27, jnp.zeros((32, L), BF)], axis=0))
             rtf = rt.astype(F32)
             centre = rtf[:, 13:14] + (rtf[:, 45:46] + rtf[:, 77:78])
-            rel = []
             for d in range(3):
                 sl = slice(16 * d, 16 * d + 16)
-                rel.append(
-                    jnp.sum(jnp.where(m_slot, got[sl], 0.0) - jnp.where(m_s, centre[sl], 0.0), axis=0, keepdims=True)
+                geo_sc[gi, d, j : j + 1, :] = jnp.sum(
+                    jnp.where(m_slot, got[sl], 0.0) - jnp.where(m_s, centre[sl], 0.0), axis=0, keepdims=True
                 )
-            rx, ry, rz = rel
-            d2, inv, dist, nx, ny, nz = sphere(rx, ry, rz)
-            u = jnp.maximum(1.0 - d2 * (1.0 / 144.0), 0.0)
-            w = live * (u * u)
-            arg = (dist - (0.5 + 2.0 * iota((8, L), 0, F32))) * 0.5
+
+        weave(find(j, i, c) for j, (i, c) in enumerate(zip(ids, cells)))
+        rx, ry, rz, d2, inv, dist, nx, ny, nz = sphere(gi)
+        u = jnp.maximum(1.0 - d2 * (1.0 / 144.0), 0.0)
+        geo_sc[gi, WEIGHT] = geo_sc[gi, LIVE] * (u * u)
+        y_sc[0] = dist
+        y_sc[1] = nx
+        y_sc[2] = ny
+        y_sc[3] = nz
+        y_sc[4] = root_three * nx * ny
+        y_sc[5] = root_three * ny * nz
+        y_sc[6] = 0.5 * (3.0 * nz * nz - 1.0)
+        y_sc[7] = root_three * nx * nz
+        y_sc[8] = (0.5 * root_three) * (nx * nx - ny * ny)
+
+        def layers(j, i, c):
+            x = lax.div(c, CY * CZ)
+            rest = c - x * (CY * CZ)
+            y = lax.div(rest, CZ)
+            z = rest - y * CZ
+            parts = [
+                proj_sc[pl.ds(((x + k // 3) * EY + y + k % 3) * EZ + z, 3)].reshape(48, 128) for k in range(9)
+            ]
+            parts.append(mats[3, 48:64, :])
+            tab = jnp.concatenate(parts, axis=0)
+            code, slot, s = [geo_sc[gi, q, j : j + 1, :] for q in (CODE, SLOT, WHO)]
+            arg = (y_sc[0, j : j + 1, :] - centres) * 0.5
             basis = jnp.exp(-(arg * arg))
-            slot01 = onoff(m_slot).astype(BF)
-            s01 = onoff(m_s).astype(BF)
+            slot01 = onoff(slot == sub16).astype(BF)
+            s01 = onoff(s == sub16).astype(BF)
             code16 = rows16(code)
             tiles = [jnp.where(code16 == float(k), slot01, zero) for k in range(27)]
             tiles[13] = tiles[13] + s01
             tiles.append(jnp.concatenate([basis, jnp.zeros((8, L), F32)], axis=0).astype(BF))
-            pres.append(nn(tab, jnp.concatenate(tiles + [zero] * 4, axis=0)))
-            ylist = [
-                nx, ny, nz, root_three * nx * ny, root_three * ny * nz,
-                0.5 * (3.0 * nz * nz - 1.0), root_three * nx * nz, (0.5 * root_three) * (nx * nx - ny * ny),
-            ]
-            ys = jnp.concatenate([s01] + [s01 * rows16(v) for v in ylist], axis=0)
-            geo = jnp.concatenate([rx, ry, rz, live, code, slot, s, w], axis=0)
-            rest.append((ys, geo, rows16(w)))
-        firsts = [silu_both(v) for v in pres]
-        secs = [silu_both(nn(mats[1], f.astype(BF))) for f, _ in firsts]
-        qs = []
-        for (sec, d), (ys, geo, w16) in zip(secs, rest):
+            pre = tn(tab, jnp.concatenate(tiles, axis=0))
+            yield 1
+            f, d1 = silu_both(pre)
+            d1_sc[i] = d1.astype(BF)
+            hidden = nn(mats[1], f.astype(BF))
+            yield 1
+            ys = jnp.concatenate([s01] + [s01 * rows16(y_sc[m, j : j + 1, :]) for m in range(1, 9)], axis=0)
+            ys_sc[i] = ys
+            sec, d2 = silu_both(hidden)
+            d2_sc[i] = d2.astype(BF)
             sb = sec.astype(BF)
-            qs.append((sb, nt(ys * jnp.concatenate([w16] * 9, axis=0), sb)))
-        for i, c, (f, d1), (sec, d2), (ys, geo, w16), (sb, q) in zip(ids, cells, firsts, secs, rest, qs):
             sec_sc[i] = sb
-            d1_sc[i] = d1.astype(BF)
-            d2_sc[i] = d2.astype(BF)
-            ys_sc[i] = ys
-            geo_sc[i] = geo
+            w16 = rows16(geo_sc[gi, WEIGHT, j : j + 1, :])
+            q = nt(ys * jnp.concatenate([w16] * 9, axis=0), sb)
+            yield 1
             q_sc[:, c] = q_sc[:, c] + q.reshape(9, 16, 128)
+
+        weave(layers(j, i, c) for j, (i, c) in enumerate(zip(ids, cells)))
         return 0
 
     lax.fori_loop(0, groups, front, 0)
@@ -266,24 +306,33 @@
         ids, cells = ids_of(gi)
         wout = jnp.concatenate([wout_b[...]] * (L // 128), axis=1)
         wout_h = 0.5 * wout
-        mts = [nt(ident, m_sc[:, c].reshape(144, 128)).astype(BF) for c in cells]
-        yss = [ys_sc[i] for i in ids]
-        ps = [nn(mats[2], sec_sc[i]) + nn(mt, ys) for i, mt, ys in zip(ids, mts, yss)]
-        outs = []
-        for i, p, ys in zip(ids, ps, yss):
-            w = geo_sc[i, 7:8, :]
+        row = iota((16, 128), 0)
+        w_hi = wout_r[0:1, :].astype(BF).astype(F32)
+        w_rows = jnp.where(row == 0, w_hi, jnp.where(row == 1, wout_r[0:1, :] - w_hi, 0.0)).astype(BF)
+
+        def mix(j, i, c):
+            mt = nt(ident, m_sc[:, c].reshape(144, 128)).astype(BF)
+            yield 1
+            ys = ys_sc[i]
+            p = nn(mats[2], sec_sc[i]) + nn(mt, ys)
+            yield 1
+            w = geo_sc[gi, WEIGHT, j : j + 1, :]
             mixed, d = silu_both(p)
-            eps = jnp.sum(mixed * wout, axis=0, keepdims=True)
             g = (d * wout_h).astype(BF)
+            g_sc[i] = g
+            energies = nn(w_rows, mixed.astype(BF))
+            dm = nt(ys * jnp.concatenate([rows16(w)] * 9, axis=0), g)
+            yield 1
+            eps = energies[0:1] + energies[1:2]
+            geo_sc[gi, EPS, j : j + 1, :] = eps
             we = eps * w
             hi = we.astype(BF).astype(F32)
             en = nt(jnp.where(iota((16, L), 0) == 0, hi, jnp.where(iota((16, L), 0) == 1, we - hi, 0.0)).astype(BF), ys[0:16])
-            outs.append((eps, g, en, nt(ys * jnp.concatenate([rows16(w)] * 9, axis=0), g)))
-        for i, c, (eps, g, en, dm) in zip(ids, cells, outs):
-            g_sc[i] = g
-            eps_sc[i] = eps
             dm_sc[:, c] = dm_sc[:, c] + dm.reshape(9, 16, 128)
+            yield 1
             en_sc[c] = en_sc[c] + en[0:8]
+
+        weave(mix(j, i, c) for j, (i, c) in enumerate(zip(ids, cells)))
         return 0
 
     lax.fori_loop(0, groups, middle, 0)
@@ -294,53 +343,66 @@
 
     def back(gi, _):
         ids, cells = ids_of(gi)
-        dqs = [dq_sc[:, c].reshape(144, 128) for c in cells]
-        dqts = [nt(ident, v).astype(BF) for v in dqs]
-        secs = [sec_sc[i] for i in ids]
-        ts = [nn(v, ys_sc[i]) for i, v in zip(ids, dqts)]
-        dpres, dys, dws = [], [], []
         top = jnp.concatenate([w_mix[0:128, :], jnp.zeros((128, 128), BF)], axis=1)
-        for i, c, sb, t, dq in zip(ids, cells, secs, ts, dqs):
+        col, row = iota((16, 256), 1), iota((16, 256), 0)
+        part = jnp.where(col < 128, 0, lax.shift_right_logical(col - 128, 4) + 1)
+        gather = onoff(part == row).astype(BF)
+        rx, ry, rz, d2, inv, dist, nx, ny, nz = sphere(gi)
+        y_sc[0] = dist
+
+        def undo(j, i, c):
+            dq = dq_sc[:, c].reshape(144, 128)
+            dqt = nt(ident, dq).astype(BF)
+            yield 1
+            t = nn(dqt, ys_sc[i])
+            sb = sec_sc[i]
+            low = jnp.concatenate([m_sc[1:9, c].reshape(128, 128), dq[16:144]], axis=1)
+            both = nn(jnp.concatenate([top, low], axis=0), jnp.concatenate([g_sc[i], sb], axis=0))
+            yield 1
             t2 = t + t
-            low = jnp.concatenate([m_sc[:, c].reshape(144, 128), dq], axis=1)
-            both = nn(jnp.concatenate([top, low], axis=0), jnp.concatenate([g_sc[i], sb], axis=0))
             dsec = both[0:128] + t2
-            dws.append(eps_sc[i] + jnp.sum(sb.astype(F32) * t2, axis=0, keepdims=True))
-            dys.append(both[128:272])
-            dfirst = nn(w_hid[...], (dsec * d2_sc[i].astype(F32)).astype(BF))
-            dpres.append((dfirst * d1_sc[i].astype(F32)).astype(BF))
-        adds = []
-        for i, dpre, dyf, dw in zip(ids, dpres, dys, dws):
-            dbasis = nn(mats[3, 48:64, :], dpre)[0:8]
-            geo = geo_sc[i]
-            rx, ry, rz, live, code, slot, s, w = [geo[j : j + 1] for j in range(8)]
-            d2, inv, dist, nx, ny, nz = sphere(rx, ry, rz)
-            m_slot = slot == sub16
-            m_s = s == sub16
-            w2 = w + w
-            dy = [
-                jnp.sum(jnp.where(m_s, dyf[16 * m : 16 * m + 16], 0.0), axis=0, keepdims=True) * w2 for m in range(1, 9)
-            ]
-            y1, y2, y3, y4, y5, y6, y7, y8 = dy
-            ax = y1 + root_three * (ny * y4 + nz * y7 + nx * y8)
-            ay = y2 + root_three * (nx * y4 + nz * y5 - ny * y8)
-            az = y3 + root_three * (ny * y5 + nx * y7) + 3.0 * nz * y6
-            arg = (dist - (0.5 + 2.0 * iota((8, L), 0, F32))) * 0.5
-            basis = jnp.exp(-(arg * arg))
-            dd = jnp.sum(dbasis * basis * arg, axis=0, keepdims=True) * (-0.25 * w)
-            dd = dd - (ax * nx + ay * ny + az * nz) * inv
-            u = jnp.maximum(1.0 - d2 * (1.0 / 144.0), 0.0)
-            radial = dd * inv + dw * live * u * (-4.0 / 144.0)
-            grads = [a * inv + r * radial for a, r in ((ax, rx), (ay, ry), (az, rz))]
-            slot01 = onoff(m_slot).astype(BF)
-            s01 = onoff(m_s).astype(BF)
-            g16 = [rows16(v) for v in grads]
+            dfirst = nn(w_hid[...], dsec.astype(BF) * d2_sc[i])
+            s01 = onoff(geo_sc[gi, WHO, j : j + 1, :] == sub16).astype(BF)
+            sums = nn(
+                gather,
+                jnp.concatenate([t2.astype(BF) * sb, both[128:256].astype(BF) * jnp.concatenate([s01] * 8, axis=0)], axis=0),
+            )
+            yield 1
+            for m in range(9):
+                red_sc[m, j : j + 1, :] = sums[m : m + 1]
+            dbasis = nn(mats[3, 48:64, :], dfirst.astype(BF) * d1_sc[i])[0:8]
+            yield 1
+            arg = (y_sc[0, j : j + 1, :] - centres) * 0.5
+            red_sc[9, j : j + 1, :] = jnp.sum(dbasis * jnp.exp(-(arg * arg)) * arg, axis=0, keepdims=True)
+
+        weave(undo(j, i, c) for j, (i, c) in enumerate(zip(ids, cells)))
+        w = geo_sc[gi, WEIGHT]
+        w2 = w + w
+        dw = geo_sc[gi, EPS] + red_sc[0]
+        y1, y2, y3, y4, y5, y6, y7, y8 = [red_sc[m] * w2 for m in range(1, 9)]
+        ax = y1 + root_three * (ny * y4 + nz * y7 + nx * y8)
+        ay = y2 + root_three * (nx * y4 + nz * y5 - ny * y8)
+        az = y3 + root_three * (ny * y5 + nx * y7) + 3.0 * nz * y6
+        dd = red_sc[9] * (-0.5 * w) - (ax * nx + ay * ny + az * nz) * inv
+        u = jnp.maximum(1.0 - d2 * (1.0 / 144.0), 0.0)
+        radial = dd * inv + dw * geo_sc[gi, LIVE] * u * (-4.0 / 144.0)
+        gr_sc[0] = ax * inv + rx * radial
+        gr_sc[1] = ay * inv + ry * radial
+        gr_sc[2] = az * inv + rz * radial
+        where32 = iota((32, L), 0, F32)
+
+        def scatter(j, i, c):
+            code, slot, s = [geo_sc[gi, q, j : j + 1, :] for q in (CODE, SLOT, WHO)]
+            slot01 = onoff(slot == sub16).astype(BF)
+            s01 = onoff(s == sub16).astype(BF)
+            g16 = [rows16(gr_sc[d, j : j + 1, :]) for d in range(3)]
             parts = [slot01 * -v for v in g16] + [zero] + [s01 * v for v in g16] + [zero]
-            where32 = iota((32, L), 0, F32)
             oh = onoff((code == where32) | (where32 == 27.0)).astype(BF)
-            adds.append(nt(oh, jnp.concatenate(parts, axis=0)))
-        for c, f in zip(cells, adds):
-            f_sc[c] = f_sc[c] + f
+            add = nt(oh, jnp.concatenate(parts, axis=0))
+            yield 1
+            f_sc[c] = f_sc[c] + add
+
+        weave(scatter(j, i, c) for j, (i, c) in enumerate(zip(ids, cells)))
         return 0
 
     lax.fori_loop(0, groups, back, 0)
@@ -370,13 +432,13 @@
     jax.ShapeDtypeStruct((CELLS, 48, 128), BF),
     jax.ShapeDtypeStruct((8, 128), I32),
     jax.ShapeDtypeStruct((7, 128, 128), BF),
-    jax.ShapeDtypeStruct((128, 128), F32),
+    jax.ShapeDtypeStruct((8, 128), F32),
     jax.ShapeDtypeStruct((128, 128), F32),
 )
 
 
 def edge_stage(feats, prepared, w_mix, w_hid):
-    rank, code, rt, todo, mats, radpad, wout_b = prepared
+    rank, code, rt, todo, mats, wout_r, wout_b = prepared
     V = pltpu.VMEM
     vm = pl.BlockSpec(memory_space=pltpu.VMEM)
     folds = fold_matrices()
@@ -386,6 +448,7 @@
         in_specs=[pl.BlockSpec(memory_space=pltpu.SMEM)] + [vm] * 11,
         out_specs=(vm, vm),
         scratch_shapes=[
+            V((GHOSTED, 16, 128), BF),
             V((9, CELLS, 16, 128), F32),
             V((9, CELLS, 16, 128), F32),
             V((9, CELLS, 16, 128), BF),
@@ -397,12 +460,14 @@
             V((MAXCH, 128, L), BF),
             V((MAXCH, 128, L), BF),
             V((MAXCH, 144, L), BF),
-            V((MAXCH, 8, L), F32),
-            V((MAXCH, 1, L), F32),
+            V((MAXCH // G, 9, G, L), F32),
+            V((9, G, L), F32),
+            V((10, G, L), F32),
+            V((3, G, L), F32),
         ],
         compiler_params=pltpu.CompilerParams(vmem_limit_bytes=60 * 1024 * 1024),
         name="edges",
-    )(todo, feats, rank, code, rt, mats, radpad, wout_b, w_mix, w_hid, jnp.asarray(folds[0], BF), jnp.asarray(folds[1], BF))
+    )(todo, feats, rank, code, rt, mats, wout_r, wout_b, w_mix, w_hid, jnp.asarray(folds[0], BF), jnp.asarray(folds[1], BF))
 
 
 MESH = pl.DeviceIdType.MESH
@@ -442,7 +507,7 @@
 
 def halo_kernel(
     occ_s, pos, feat, neigh, counts, w_atom, w_rad, w_hid, w_ten_t, w_mix, w_out,
-    feat_ext, rank, code, rt, todo, mats, radpad, wout_b,
+    feat_ext, rank, code, rt, todo, mats, wout_r, wout_b,
     rows, rows2, occ_sp, send, recv,
 ):
     barrier = greet()
@@ -479,7 +544,7 @@
     for copy in feat_z:
         copy.wait()
     feat_xy = around(feat_ext, 12)
-    prepare_weights(w_atom, w_rad, w_hid, w_ten_t, w_mix, w_out, mats, radpad, wout_b)
+    prepare_weights(w_atom, w_rad, w_hid, w_ten_t, w_mix, w_out, mats, wout_r, wout_b)
     for copy in rows_xy:
         copy.wait()
     prepare_edges(rows, rows2, occ_sp, neigh, counts, rank, code, rt, todo)
@@ -503,7 +568,7 @@
             pltpu.SemaphoreType.DMA((20,)),
         ],
         compiler_params=pltpu.CompilerParams(
-            collective_id=0, has_side_effects=True, vmem_limit_bytes=32 * 1024 * 1024
+            collective_id=0, has_side_effects=True, vmem_limit_bytes=60 * 1024 * 1024
         ),
         name="halo",
     )(occ, pos, feat, neigh, counts, w_atom, w_rad, w_hid, w_ten_t, w_mix, w_out)
@@ -567,7 +632,7 @@
             pltpu.SemaphoreType.DMA((10,)),
             pltpu.SemaphoreType.DMA((10,)),
         ],
-        compiler_params=pltpu.CompilerParams(collective_id=1, has_side_effects=True),
+        compiler_params=pltpu.CompilerParams(collective_id=1, has_side_effects=True, vmem_limit_bytes=60 * 1024 * 1024),
         name="fold",
     )(grid)
 

time: 93.3 us -> 65 us (0.70)
  Pallas kernels: 78.1 us -> 62.7 us
  local copies, waits for them, and re-layouts: 13.9 us -> 1.42 us
    pallas_call x1, Pallas kernels: 39.6 us -> 26.3 us  [edge_stage(): pl.pallas_call(edge_kernel, out_shape=(jax.ShapeDtypeStruct((CELLS, 16),...]
    unnamed x39 -> x1, local copies, waits for them, and re-layouts: 13.9 us -> 1.42 us
    pallas_call x1, Pallas kernels: 16.2 us -> 12.3 us  [fold_stage(): pl.pallas_call(fold_kernel, out_shape=jax.ShapeDtypeStruct((3, CELLS, 16)...]
    pallas_call x1, Pallas kernels: 22.3 us -> 24.1 us  [halo_stage(): pl.pallas_call(halo_kernel, out_shape=(jax.ShapeDtypeStruct((EX, EY, EZ,...]
where the time goes in v2:
time: 65 us; the launch traced here: 64.7 us
  Pallas kernels  62.7 us (96%)
  local copies, waits for them, and re-layouts  1.42 us (2%)
  between operations  0.65 us (1%)
    pallas_call x1, Pallas kernels, edge_stage(): pl.pallas_call(edge_kernel, out_shape=(jax.ShapeDtypeStruct((CELLS, 16),...  26.3 us
    pallas_call x1, Pallas kernels, halo_stage(): pl.pallas_call(halo_kernel, out_shape=(jax.ShapeDtypeStruct((EX, EY, EZ,...  24.1 us
    pallas_call x1, Pallas kernels, fold_stage(): pl.pallas_call(fold_kernel, out_shape=jax.ShapeDtypeStruct((3, CELLS, 16)...  12.3 us
    unnamed x1, local copies, waits for them, and re-layouts  1.42 us

profile of v2, /device:TPU:1, one launch (start us, length us, event | category | flops | bytes accessed | tf_op | source)
XLA Modules:
  0.0 64.7 jit_solution(8242685772333300497)
XLA Ops:
  0.6 24.1 %halo.1 = (bf16[6,6,4,16,128]{4,3,2,1,0:T(8,128)(2,1)}, s32[32,8,128]{2,1,0:T(8,128)}, s32[32,8,128]{2,1,0:T(8,128)}, bf16[32,48,128]{2,1,0:T(8,128)(2,1)}, s32[...) custom-call(s32[4,2,4]{2,1,0:T(2,128)} %bitcast.19, ...), custom_call_target="tpu_custom_call" | custom-call | tf_op jit(solution)/shard_map/halo/pallas_call | solution.py:558
  24.7 26.3 %edges.1 = (f32[32,16]{1,0:T(8,128)}, f32[144,128]{1,0:T(8,128)}) custom-call(s32[8,128]{1,0:T(8,128)} %get-tuple-element.12.list_s, bf16[144,16,128]{2,1,0:T(8,128)(2,1)} %bitcast.11, s32[32,8,128]{2,1,0:T(8,128)} %get-tuple-element.14.rank_r, s32[32,8,128]{2,1,0:T(8,128)} %get-tuple-element.15.code_r, bf16[32,48,128]{2,1,0:T(8,128)(2,1)} %get-tuple-element.16.rt_r, ...), custom_call_target="tpu_custom_call" | custom-call | tf_op jit(solution)/shard_map/edges/pallas_call | solution.py:445
  51.0 12.3 %fold.2 = f32[3,32,16]{2,1,0:T(8,128)} custom-call(f32[6,6,4,1,128]{4,3,2,1,0:T(1,128)} %bitcast.15), custom_call_target="tpu_custom_call" | custom-call | tf_op jit(solution)/shard_map/fold/pallas_call | solution.py:621
  63.3 1.4 %copy.16 = f32[3,4,4,2,16]{4,3,2,1,0:T(2,128)} copy(f32[3,4,4,2,16]{4,3,2,1,0:T(2,128)} %bitcast.13) | data formatting | bytes 12288

commit v3 on v2

--- a/solution.py
+++ b/solution.py
@@ -11,12 +11,14 @@
 I32 = jnp.int32
 root_three = 1.7320508075688772
 L = 256
-G = 8
+G = 12
 CX, CY, CZ = 4, 4, 2
 EX, EY, EZ = CX + 2, CY + 2, CZ + 2
 CELLS = CX * CY * CZ
 GHOSTED = EX * EY * EZ
-MAXCH = CELLS * (1024 // L)
+MAXGR = -(-CELLS * (1024 // L) // G)
+MAXCH = MAXGR * G
+LISTED = 256
 
 
 def nn(a, b):
@@ -109,13 +111,14 @@
     n = (base + total).reshape(CELLS, 8, 128)[:, 7, :].astype(I32)
     chunks = lax.shift_right_logical(n + (L - 1), L.bit_length() - 1).astype(F32)
     ends = nn(onoff(iota((CELLS, CELLS), 1) <= iota((CELLS, CELLS), 0)).astype(BF), chunks.astype(BF))
-    t = iota((CELLS, 128), 1, F32)
+    ends = jnp.concatenate([ends] * (LISTED // 128), axis=1)
+    t = iota((CELLS, LISTED), 1, F32)
     done = ends <= t
     cell = jnp.minimum(jnp.sum(onoff(done), axis=0, keepdims=True), CELLS - 1.0)
     start = jnp.max(jnp.where(done, ends, 0.0), axis=0, keepdims=True)
     all_of = ends[CELLS - 1 : CELLS]
     first = jnp.where(t[0:1] < all_of, (t[0:1] - start) * L, 4096.0)
-    list_out[...] = jnp.concatenate([cell, first, all_of, jnp.zeros((5, 128), F32)], axis=0).astype(I32)
+    list_out[...] = jnp.concatenate([cell, first, all_of, jnp.zeros((5, LISTED), F32)], axis=0).astype(I32)
 
     lane = iota((32, 128), 1)
     code_i = iota((32, 128), 0)
@@ -144,9 +147,9 @@
 
 def silu_both(h):
     t = jnp.tanh(h)
-    a = 1.0 + t
-    y = h * a
-    return y, a + y * (1.0 - t)
+    y = (h + h * t).astype(BF)
+    t = t.astype(BF)
+    return y, (1.0 + t) + y * (1.0 - t)
 
 
 def wide16(v):
@@ -167,14 +170,16 @@
 
 
 def edge_kernel(
-    list_s, feats, rank_r, code_r, rt_r, mats, wout_r, wout_b, w_mix, w_hid, fold, foldc,
+    list_s, feats, rank_r, code_r, rt_r, mats, wout_r, wout_b, w_mix, w_hid, fold_h,
     energy_out, force_out,
-    proj_sc, q_sc, dm_sc, m_sc, dq_sc, f_sc, en_sc, sec_sc, d1_sc, d2_sc, g_sc, ys_sc, geo_sc, y_sc, red_sc, gr_sc,
+    proj_sc, q_sc, m_sc, dq_sc, f_sc, en_sc, sec_sc, d1_sc, d2_sc, g_sc, ys_sc, geo_sc, y_sc, red_sc, gr_sc,
+    fold, fold_sem,
 ):
+    fold_copy = pltpu.make_async_copy(fold_h, fold, fold_sem)
+    fold_copy.start()
     groups = lax.div(list_s[2, 0] + (G - 1), G)
     ident = eye(128, 128)
     q_sc[...] = jnp.zeros_like(q_sc)
-    dm_sc[...] = jnp.zeros_like(dm_sc)
     f_sc[...] = jnp.zeros_like(f_sc)
     en_sc[...] = jnp.zeros_like(en_sc)
     sub16 = iota((16, L), 0, F32)
@@ -198,7 +203,8 @@
         lane_l = iota((16, L), 1)
         unfold = onoff(lax.bitwise_and(lane_l, 15) == iota((16, L), 0)).astype(BF)
         in_high = lax.shift_right_logical(lane_l, 4) == iota((16, L), 0)
-        s_lane = iota((1, 128), 1)
+        lane8 = iota((8, 128), 1)
+        s_of = jnp.where(lane8 < 64, iota((8, 128), 0), iota((8, 128), 0) + 8)
         ones = jnp.ones((16, 128), BF)
         zeros = jnp.zeros((16, 128), BF)
 
@@ -208,25 +214,26 @@
             high = jnp.where(inside, lax.shift_right_logical(rk, 4), -1).astype(F32)
             deep = lax.bitwise_and(rk, 15).astype(F32)
             nb = code_r[c]
-            code_f = lax.shift_right_logical(nb, 4).astype(F32)
-            slot_f = lax.bitwise_and(nb, 15).astype(F32)
+            code_f = (lax.shift_right_logical(nb, 4) + 1).astype(F32)
+            pair_f = (lax.bitwise_and(nb, 15) + 16 * s_of).astype(F32)
             left, right = [], []
             for k in range(8):
-                s_row = jnp.where(s_lane < 64, float(k), float(k + 8))
                 at_high = jnp.where(sixteen == wide16(high[k : k + 1]), ones, zeros)
                 left.append(
-                    jnp.concatenate(
-                        [at_high * wide16(v) for v in (code_f[k : k + 1], slot_f[k : k + 1], s_row)] + [at_high], axis=0
-                    )
+                    jnp.concatenate([at_high * wide16(code_f[k : k + 1]), at_high * wide16(pair_f[k : k + 1])], axis=0)
                 )
                 right.append(jnp.where(sixteen == wide16(deep[k : k + 1]), ones, zeros))
             packed = nt(jnp.concatenate(left, axis=1), jnp.concatenate(right, axis=1))
             yield 1
             spread = nn(packed.astype(BF), unfold)
             yield 1
-            code, slot, s, live = [
-                jnp.sum(jnp.where(in_high, spread[16 * a : 16 * a + 16], 0.0), axis=0, keepdims=True) for a in range(4)
+            code1, pair = [
+                jnp.sum(jnp.where(in_high, spread[16 * a : 16 * a + 16], 0.0), axis=0, keepdims=True) for a in range(2)
             ]
+            live = jnp.minimum(code1, 1.0)
+            code = code1 - live
+            s = jnp.floor(pair * 0.0625)
+            slot = pair - 16.0 * s
             oh27 = onoff(code == iota((32, L), 0, F32)).astype(BF)
             rt = rt_r[c]
             got = nn(rt, jnp.concatenate([oh27, oh27, oh27, jnp.zeros((32, L), BF)], axis=0))
@@ -279,14 +286,13 @@
             pre = tn(tab, jnp.concatenate(tiles, axis=0))
             yield 1
             f, d1 = silu_both(pre)
-            d1_sc[i] = d1.astype(BF)
-            hidden = nn(mats[1], f.astype(BF))
+            d1_sc[i] = d1
+            hidden = nn(mats[1], f)
             yield 1
             ys = jnp.concatenate([s01] + [s01 * rows16(y_sc[m, j : j + 1, :]) for m in range(1, 9)], axis=0)
-            ys_sc[i] = ys
-            sec, d2 = silu_both(hidden)
-            d2_sc[i] = d2.astype(BF)
-            sb = sec.astype(BF)
+            ys_sc[i] = ys[16:144]
+            sb, d2 = silu_both(hidden)
+            d2_sc[i] = d2
             sec_sc[i] = sb
             w16 = rows16(geo_sc[gi, WEIGHT, j : j + 1, :])
             q = nt(ys * jnp.concatenate([w16] * 9, axis=0), sb)
@@ -301,26 +307,25 @@
     for m in range(9):
         l = 0 if m == 0 else 1 if m < 4 else 2
         m_sc[m] = nn(q_sc[m].reshape(CELLS * 16, 128).astype(BF), mats[4 + l]).astype(BF).reshape(CELLS, 16, 128)
+        q_sc[m] = jnp.zeros((CELLS, 16, 128), F32)
 
     def middle(gi, _):
         ids, cells = ids_of(gi)
-        wout = jnp.concatenate([wout_b[...]] * (L // 128), axis=1)
-        wout_h = 0.5 * wout
+        wout_h = jnp.concatenate([(0.5 * wout_b[...]).astype(BF)] * (L // 128), axis=1)
         row = iota((16, 128), 0)
         w_hi = wout_r[0:1, :].astype(BF).astype(F32)
         w_rows = jnp.where(row == 0, w_hi, jnp.where(row == 1, wout_r[0:1, :] - w_hi, 0.0)).astype(BF)
 
         def mix(j, i, c):
-            mt = nt(ident, m_sc[:, c].reshape(144, 128)).astype(BF)
-            yield 1
-            ys = ys_sc[i]
-            p = nn(mats[2], sec_sc[i]) + nn(mt, ys)
+            s01 = onoff(geo_sc[gi, WHO, j : j + 1, :] == sub16).astype(BF)
+            ys = jnp.concatenate([s01, ys_sc[i]], axis=0)
+            p = nn(mats[2], sec_sc[i]) + tn(m_sc[:, c].reshape(144, 128), ys)
             yield 1
             w = geo_sc[gi, WEIGHT, j : j + 1, :]
             mixed, d = silu_both(p)
-            g = (d * wout_h).astype(BF)
+            g = d * wout_h
             g_sc[i] = g
-            energies = nn(w_rows, mixed.astype(BF))
+            energies = nn(w_rows, mixed)
             dm = nt(ys * jnp.concatenate([rows16(w)] * 9, axis=0), g)
             yield 1
             eps = energies[0:1] + energies[1:2]
@@ -328,7 +333,7 @@
             we = eps * w
             hi = we.astype(BF).astype(F32)
             en = nt(jnp.where(iota((16, L), 0) == 0, hi, jnp.where(iota((16, L), 0) == 1, we - hi, 0.0)).astype(BF), ys[0:16])
-            dm_sc[:, c] = dm_sc[:, c] + dm.reshape(9, 16, 128)
+            q_sc[:, c] = q_sc[:, c] + dm.reshape(9, 16, 128)
             yield 1
             en_sc[c] = en_sc[c] + en[0:8]
 
@@ -339,7 +344,7 @@
 
     for m in range(9):
         l = 0 if m == 0 else 1 if m < 4 else 2
-        dq_sc[m] = nt(dm_sc[m].reshape(CELLS * 16, 128).astype(BF), mats[4 + l]).astype(BF).reshape(CELLS, 16, 128)
+        dq_sc[m] = nt(q_sc[m].reshape(CELLS * 16, 128).astype(BF), mats[4 + l]).astype(BF).reshape(CELLS, 16, 128)
 
     def back(gi, _):
         ids, cells = ids_of(gi)
@@ -352,9 +357,8 @@
 
         def undo(j, i, c):
             dq = dq_sc[:, c].reshape(144, 128)
-            dqt = nt(ident, dq).astype(BF)
-            yield 1
-            t = nn(dqt, ys_sc[i])
+            s01 = onoff(geo_sc[gi, WHO, j : j + 1, :] == sub16).astype(BF)
+            t = tn(dq, jnp.concatenate([s01, ys_sc[i]], axis=0))
             sb = sec_sc[i]
             low = jnp.concatenate([m_sc[1:9, c].reshape(128, 128), dq[16:144]], axis=1)
             both = nn(jnp.concatenate([top, low], axis=0), jnp.concatenate([g_sc[i], sb], axis=0))
@@ -362,7 +366,6 @@
             t2 = t + t
             dsec = both[0:128] + t2
             dfirst = nn(w_hid[...], dsec.astype(BF) * d2_sc[i])
-            s01 = onoff(geo_sc[gi, WHO, j : j + 1, :] == sub16).astype(BF)
             sums = nn(
                 gather,
                 jnp.concatenate([t2.astype(BF) * sb, both[128:256].astype(BF) * jnp.concatenate([s01] * 8, axis=0)], axis=0),
@@ -407,11 +410,12 @@
 
     lax.fori_loop(0, groups, back, 0)
 
+    fold_copy.wait()
     fa = f_sc[...].reshape(CELLS * 32, 128)
     fh = fa.astype(BF)
     fl = (fa - fh.astype(F32)).astype(BF)
-    others = nn(fold[...], fh) + nn(fold[...], fl)
-    own = nn(foldc[...], fh) + nn(foldc[...], fl)
+    others = nn(fold[0], fh) + nn(fold[0], fl)
+    own = nn(fold[1], fh) + nn(fold[1], fl)
     force_out[...] = others + jnp.concatenate([own[:, 64:128], jnp.zeros((GHOSTED, 64), F32)], axis=1)
     energy_out[...] = en_sc[:, 0, :] + en_sc[:, 1, :]
 
@@ -430,7 +434,7 @@
     jax.ShapeDtypeStruct((CELLS, 8, 128), I32),
     jax.ShapeDtypeStruct((CELLS, 8, 128), I32),
     jax.ShapeDtypeStruct((CELLS, 48, 128), BF),
-    jax.ShapeDtypeStruct((8, 128), I32),
+    jax.ShapeDtypeStruct((8, LISTED), I32),
     jax.ShapeDtypeStruct((7, 128, 128), BF),
     jax.ShapeDtypeStruct((8, 128), F32),
     jax.ShapeDtypeStruct((128, 128), F32),
@@ -441,15 +445,13 @@
     rank, code, rt, todo, mats, wout_r, wout_b = prepared
     V = pltpu.VMEM
     vm = pl.BlockSpec(memory_space=pltpu.VMEM)
-    folds = fold_matrices()
     return pl.pallas_call(
         edge_kernel,
         out_shape=(jax.ShapeDtypeStruct((CELLS, 16), F32), jax.ShapeDtypeStruct((GHOSTED, 128), F32)),
-        in_specs=[pl.BlockSpec(memory_space=pltpu.SMEM)] + [vm] * 11,
+        in_specs=[pl.BlockSpec(memory_space=pltpu.SMEM)] + [vm] * 9 + [pl.BlockSpec(memory_space=pl.ANY)],
         out_specs=(vm, vm),
         scratch_shapes=[
             V((GHOSTED, 16, 128), BF),
-            V((9, CELLS, 16, 128), F32),
             V((9, CELLS, 16, 128), F32),
             V((9, CELLS, 16, 128), BF),
             V((9, CELLS, 16, 128), BF),
@@ -459,19 +461,22 @@
             V((MAXCH, 128, L), BF),
             V((MAXCH, 128, L), BF),
             V((MAXCH, 128, L), BF),
-            V((MAXCH, 144, L), BF),
-            V((MAXCH // G, 9, G, L), F32),
+            V((MAXCH, 128, L), BF),
+            V((MAXGR, 9, G, L), F32),
             V((9, G, L), F32),
             V((10, G, L), F32),
             V((3, G, L), F32),
+            V((2, GHOSTED, CELLS * 32), BF),
+            pltpu.SemaphoreType.DMA,
         ],
         compiler_params=pltpu.CompilerParams(vmem_limit_bytes=60 * 1024 * 1024),
         name="edges",
-    )(todo, feats, rank, code, rt, mats, wout_r, wout_b, w_mix, w_hid, jnp.asarray(folds[0], BF), jnp.asarray(folds[1], BF))
+    )(todo, feats, rank, code, rt, mats, wout_r, wout_b, w_mix, w_hid, jnp.asarray(fold_matrices(), BF))
 
 
 MESH = pl.DeviceIdType.MESH
-AROUND = tuple((dx, dy) for dx in (-1, 0, 1) for dy in (-1, 0, 1) if (dx, dy) != (0, 0))
+STEPS = (0, -1, 1)
+AROUND = tuple((dx, dy, dz) for dx in STEPS for dy in STEPS for dz in STEPS)[1:]
 
 
 def peer(dx, dy, dz):
@@ -484,7 +489,7 @@
 
 def greet():
     barrier = pltpu.get_barrier_semaphore()
-    for dx, dy, dz in [(0, 0, -1), (0, 0, 1)] + [(dx, dy, 0) for dx, dy in AROUND]:
+    for dx, dy, dz in AROUND:
         pl.semaphore_signal(barrier, inc=1, device_id=peer(dx, dy, dz), device_id_type=MESH)
     return barrier
 
@@ -506,106 +511,110 @@
 
 
 def halo_kernel(
-    occ_s, pos, feat, neigh, counts, w_atom, w_rad, w_hid, w_ten_t, w_mix, w_out,
-    feat_ext, rank, code, rt, todo, mats, wout_r, wout_b,
-    rows, rows2, occ_sp, send, recv,
+    occ_s, pos, feat, counts, w_out, neigh_h, w_atom_h, w_rad_h, w_hid_h, w_ten_h, w_mix_h,
+    feat_ext, rank_h, code_h, rt_h, todo_h, mats_h, wout_r_h, wout_b_h,
+    w_atom, w_rad, w_hid, w_ten_t, w_mix, neigh, rank, code, rt, todo, mats, wout_r, wout_b,
+    rows, rows2, occ_sp, send, recv, inward, outward,
 ):
     barrier = greet()
+    fetched = [
+        pltpu.make_async_copy(far, near, inward.at[j])
+        for j, (far, near) in enumerate(
+            zip((w_atom_h, w_rad_h, w_hid_h, w_ten_h, w_mix_h, neigh_h), (w_atom, w_rad, w_hid, w_ten_t, w_mix, neigh))
+        )
+    ]
+    for copy in fetched:
+        copy.start()
     table = jnp.concatenate([pos[0], pos[1], pos[2], jnp.zeros((CELLS, 80), F32)], axis=1)
     lane = iota((1, 128), 1)
     for c in range(CELLS):
         x, y, z = place_of(c)
         rows[x + 1, y + 1, z + 1] = jnp.where(lane < 48, table[c : c + 1], occ_s[x, z, y].astype(F32))
         feat_ext[x + 1, y + 1, z + 1] = feat[c]
-    pl.semaphore_wait(barrier, 10)
-
-    def along_z(array, base):
-        copies = []
-        for j, step in enumerate((-1, 1)):
-            at = (pl.ds(1, CX), pl.ds(1, CY))
-            src = array.at[at + (border(step, CZ),)]
-            dst = array.at[at + (ghost(step, CZ),)]
-            copies.append(sent(src, dst, send.at[base + j], recv.at[base + j], peer(0, 0, step)))
-        return copies
+    pl.semaphore_wait(barrier, len(AROUND))
 
     def around(array, base):
         copies = []
-        for j, (dx, dy) in enumerate(AROUND):
-            src = array.at[border(dx, CX), border(dy, CY)]
-            dst = array.at[ghost(dx, CX), ghost(dy, CY)]
-            copies.append(sent(src, dst, send.at[base + j], recv.at[base + j], peer(dx, dy, 0)))
+        for j, (dx, dy, dz) in enumerate(AROUND):
+            src = array.at[border(dx, CX), border(dy, CY), border(dz, CZ)]
+            dst = array.at[ghost(dx, CX), ghost(dy, CY), ghost(dz, CZ)]
+            copies.append(sent(src, dst, send.at[base + j], recv.at[base + j], peer(dx, dy, dz)))
         return copies
 
-    rows_z = along_z(rows, 0)
-    feat_z = along_z(feat_ext, 2)
-    for copy in rows_z:
+    row_copies = around(rows, 0)
+    feat_copies = around(feat_ext, len(AROUND))
+    for copy in fetched:
         copy.wait()
-    rows_xy = around(rows, 4)
-    for copy in feat_z:
-        copy.wait()
-    feat_xy = around(feat_ext, 12)
     prepare_weights(w_atom, w_rad, w_hid, w_ten_t, w_mix, w_out, mats, wout_r, wout_b)
-    for copy in rows_xy:
+    for copy in row_copies:
         copy.wait()
     prepare_edges(rows, rows2, occ_sp, neigh, counts, rank, code, rt, todo)
-    for copy in feat_xy:
+    stored = [
+        pltpu.make_async_copy(near, far, outward.at[j])
+        for j, (near, far) in enumerate(
+            zip(
+                (rank, code, rt, todo, mats, wout_r, wout_b),
+                (rank_h, code_h, rt_h, todo_h, mats_h, wout_r_h, wout_b_h),
+            )
+        )
+    ]
+    for copy in stored:
+        copy.start()
+    for copy in feat_copies:
+        copy.wait()
+    for copy in stored:
         copy.wait()
 
 
 def halo_stage(occ, pos, feat, neigh, counts, w_atom, w_rad, w_hid, w_ten_t, w_mix, w_out):
     vm = pl.BlockSpec(memory_space=pltpu.VMEM)
     V = pltpu.VMEM
+    far = pl.BlockSpec(memory_space=pl.ANY)
+    moved = (w_atom, w_rad, w_hid, w_ten_t, w_mix, neigh)
     out = pl.pallas_call(
         halo_kernel,
         out_shape=(jax.ShapeDtypeStruct((EX, EY, EZ, 16, 128), BF),) + PREPARED,
-        in_specs=[pl.BlockSpec(memory_space=pltpu.SMEM)] + [vm] * 10,
-        out_specs=(vm,) * 8,
-        scratch_shapes=[
+        in_specs=[pl.BlockSpec(memory_space=pltpu.SMEM)] + [vm] * 4 + [far] * 6,
+        out_specs=(vm,) + (far,) * 7,
+        scratch_shapes=[V(a.shape, a.dtype) for a in moved]
+        + [V(a.shape, a.dtype) for a in PREPARED]
+        + [
             V((EX, EY, EZ, 1, 128), F32),
             V((GHOSTED, 128), F32),
             V((GHOSTED, 128), F32),
-            pltpu.SemaphoreType.DMA((20,)),
-            pltpu.SemaphoreType.DMA((20,)),
+            pltpu.SemaphoreType.DMA((2 * len(AROUND),)),
+            pltpu.SemaphoreType.DMA((2 * len(AROUND),)),
+            pltpu.SemaphoreType.DMA((6,)),
+            pltpu.SemaphoreType.DMA((7,)),
         ],
         compiler_params=pltpu.CompilerParams(
             collective_id=0, has_side_effects=True, vmem_limit_bytes=60 * 1024 * 1024
         ),
         name="halo",
-    )(occ, pos, feat, neigh, counts, w_atom, w_rad, w_hid, w_ten_t, w_mix, w_out)
+    )(occ, pos, feat, counts, w_out, neigh, w_atom, w_rad, w_hid, w_ten_t, w_mix)
     return out[0], out[1:]
 
 
-def fold_kernel(grid, out, acc, got_x, got_y, got_xy, got_z, send, recv):
+def fold_kernel(grid, out, acc, got, send, recv):
     barrier = greet()
     acc[...] = grid[...]
-    pl.semaphore_wait(barrier, 10)
+    pl.semaphore_wait(barrier, len(AROUND))
+
+    def rim(step, n):
+        return pl.ds(1, n) if step == 0 else pl.ds(0 if step < 0 else n + 1, 1)
+
+    def room(step, n):
+        return pl.ds(0, n if step == 0 else 1)
+
     copies = []
-    for j, (dx, dy) in enumerate(AROUND):
-        if dx and dy:
-            got = got_xy.at[(dx + 1) + (dy + 1) // 2]
-        elif dx:
-            got = got_x.at[(dx + 1) // 2]
-        else:
-            got = got_y.at[(dy + 1) // 2]
-        rim = (
-            pl.ds(1, CX) if dx == 0 else pl.ds(0 if dx < 0 else CX + 1, 1),
-            pl.ds(1, CY) if dy == 0 else pl.ds(0 if dy < 0 else CY + 1, 1),
-        )
-        copies.append((sent(acc.at[rim], got, send.at[j], recv.at[j], peer(dx, dy, 0)), got, dx, dy))
-    for copy, got, dx, dy in copies:
+    for j, (dx, dy, dz) in enumerate(AROUND):
+        src = acc.at[rim(dx, CX), rim(dy, CY), rim(dz, CZ)]
+        dst = got.at[j, room(dx, CX), room(dy, CY), room(dz, CZ)]
+        copies.append((sent(src, dst, send.at[j], recv.at[j], peer(dx, dy, dz)), dst))
+    for (copy, dst), (dx, dy, dz) in zip(copies, AROUND):
         copy.wait()
-        at = (border(-dx, CX), border(-dy, CY))
-        acc[at] = acc[at] + got[...]
-    inner = (pl.ds(1, CX), pl.ds(1, CY))
-    copies = []
-    for j, (step, rim) in enumerate(((-1, 0), (1, CZ + 1))):
-        copies.append(
-            sent(acc.at[inner + (pl.ds(rim, 1),)], got_z.at[j], send.at[8 + j], recv.at[8 + j], peer(0, 0, step))
-        )
-    for j, step in enumerate((-1, 1)):
-        copies[j].wait()
-        at = inner + (border(-step, CZ),)
-        acc[at] = acc[at] + got_z[j]
+        at = (border(-dx, CX), border(-dy, CY), border(-dz, CZ))
+        acc[at] = acc[at] + dst[...]
     lines = []
     for c in range(CELLS):
         x, y, z = place_of(c)
@@ -625,12 +634,9 @@
         out_specs=vm,
         scratch_shapes=[
             V((EX, EY, EZ, 1, 128), F32),
-            V((2, 1, CY, EZ, 1, 128), F32),
-            V((2, CX, 1, EZ, 1, 128), F32),
-            V((4, 1, 1, EZ, 1, 128), F32),
-            V((2, CX, CY, 1, 1, 128), F32),
-            pltpu.SemaphoreType.DMA((10,)),
-            pltpu.SemaphoreType.DMA((10,)),
+            V((len(AROUND), CX, CY, CZ, 1, 128), F32),
+            pltpu.SemaphoreType.DMA((len(AROUND),)),
+            pltpu.SemaphoreType.DMA((len(AROUND),)),
         ],
         compiler_params=pltpu.CompilerParams(collective_id=1, has_side_effects=True, vmem_limit_bytes=60 * 1024 * 1024),
         name="fold",

time: 65 us -> 58.9 us (0.906)
  Pallas kernels: 62.7 us -> 56.6 us
    pallas_call x1, Pallas kernels: 26.3 us -> 19.4 us  [edge_stage(): pl.pallas_call(edge_kernel, out_shape=(jax.ShapeDtypeStruct((CELLS, 16),...]
    pallas_call x1, Pallas kernels: 12.3 us -> 15.8 us  [fold_stage(): pl.pallas_call(fold_kernel, out_shape=jax.ShapeDtypeStruct((3, CELLS, 16)...]
    pallas_call x1, Pallas kernels: 24.1 us -> 21.4 us  [halo_stage(): pl.pallas_call(halo_kernel, out_shape=(jax.ShapeDtypeStruct((EX, EY, EZ,...]
where the time goes in v3:
time: 58.9 us; the launch traced here: 58.7 us
  Pallas kernels  56.6 us (96%)
  local copies, waits for them, and re-layouts  1.42 us (2%)
  between operations  0.66 us (1%)
    pallas_call x1, Pallas kernels, halo_stage(): pl.pallas_call(halo_kernel, out_shape=(jax.ShapeDtypeStruct((EX, EY, EZ,...  21.4 us
    pallas_call x1, Pallas kernels, edge_stage(): pl.pallas_call(edge_kernel, out_shape=(jax.ShapeDtypeStruct((CELLS, 16),...  19.4 us
    pallas_call x1, Pallas kernels, fold_stage(): pl.pallas_call(fold_kernel, out_shape=jax.ShapeDtypeStruct((3, CELLS, 16)...  15.8 us
    unnamed x1, local copies, waits for them, and re-layouts  1.42 us

profile of v3, /device:TPU:1, one launch (start us, length us, event | category | flops | bytes accessed | tf_op | source)
XLA Modules:
  0.0 58.7 jit_solution(13149217368549167451)
XLA Ops:
  0.6 21.4 %halo.1 = (bf16[6,6,4,16,128]{4,3,2,1,0:T(8,128)(2,1)}, s32[32,8,128]{2,1,0:T(8,128)}, s32[32,8,128]{2,1,0:T(8,128)}, bf16[32,48,128]{2,1,0:T(8,128)(2,1)}, s32[...) custom-call(s32[4,2,4]{2,1,0:T(2,128)} %bitcast.19, ...), custom_call_target="tpu_custom_call" | custom-call | tf_op jit(solution)/shard_map/halo/pallas_call | solution.py:574
  22.0 19.4 %edges.1 = (f32[32,16]{1,0:T(8,128)}, f32[144,128]{1,0:T(8,128)}) custom-call(s32[8,256]{1,0:T(8,128)} %get-tuple-element.12.list_s, bf16[144,16,128]{2,1,0:T(8,128)(2,1)} %bitcast.11, s32[32,8,128]{2,1,0:T(8,128)} %get-tuple-element.14.rank_r, s32[32,8,128]{2,1,0:T(8,128)} %get-tuple-element.15.code_r, bf16[32,48,128]{2,1,0:T(8,128)(2,1)} %get-tuple-element.16.rt_r, ...), custom_call_target="tpu_custom_call" | custom-call | tf_op jit(solution)/shard_map/edges/pallas_call | solution.py:448
  41.4 15.8 %fold.1 = f32[3,32,16]{2,1,0:T(8,128)} custom-call(f32[6,6,4,1,128]{4,3,2,1,0:T(1,128)} %bitcast.15), custom_call_target="tpu_custom_call" | custom-call | tf_op jit(solution)/shard_map/fold/pallas_call | solution.py:630
  57.3 1.4 %copy.15 = f32[3,4,4,2,16]{4,3,2,1,0:T(2,128)} copy(f32[3,4,4,2,16]{4,3,2,1,0:T(2,128)} %bitcast.13) | data formatting | bytes 12288

commit v4 on v3

--- a/solution.py
+++ b/solution.py
@@ -411,22 +411,26 @@
     lax.fori_loop(0, groups, back, 0)
 
     fold_copy.wait()
-    fa = f_sc[...].reshape(CELLS * 32, 128)
-    fh = fa.astype(BF)
-    fl = (fa - fh.astype(F32)).astype(BF)
-    others = nn(fold[0], fh) + nn(fold[0], fl)
-    own = nn(fold[1], fh) + nn(fold[1], fl)
-    force_out[...] = others + jnp.concatenate([own[:, 64:128], jnp.zeros((GHOSTED, 64), F32)], axis=1)
+
+    def halves(v):
+        hi = v.astype(BF)
+        return jnp.concatenate([hi, (v - hi.astype(F32)).astype(BF)], axis=1)
+
+    width = CELLS * 32
+    sums = nn(fold[:, 0:width], halves(f_sc[:, :, 0:64].reshape(width, 64)))
+    sums = sums + nn(fold[:, width : width + CELLS], halves(f_sc[:, 27, 64:128]))
+    force_out[...] = jnp.concatenate([sums[:, 0:64] + sums[:, 64:128], jnp.zeros((GHOSTED, 64), F32)], axis=1)
     energy_out[...] = en_sc[:, 0, :] + en_sc[:, 1, :]
 
 
-def fold_matrices():
-    m = np.zeros((2, GHOSTED, CELLS * 32), np.float32)
+def fold_matrix():
+    width = CELLS * 32
+    m = np.zeros((GHOSTED, width + 128), np.float32)
     for c in range(CELLS):
         x, y, z = place_of(c)
         for k in range(27):
-            m[0, ext_at(x + k // 9, y + k // 3 % 3, z + k % 3), c * 32 + k] = 1
-        m[1, ext_at(x + 1, y + 1, z + 1), c * 32 + 27] = 1
+            m[ext_at(x + k // 9, y + k // 3 % 3, z + k % 3), c * 32 + k] = 1
+        m[ext_at(x + 1, y + 1, z + 1), width + c] = 1
     return m
 
 
@@ -466,30 +470,32 @@
             V((9, G, L), F32),
             V((10, G, L), F32),
             V((3, G, L), F32),
-            V((2, GHOSTED, CELLS * 32), BF),
+            V((GHOSTED, CELLS * 32 + 128), BF),
             pltpu.SemaphoreType.DMA,
         ],
         compiler_params=pltpu.CompilerParams(vmem_limit_bytes=60 * 1024 * 1024),
         name="edges",
-    )(todo, feats, rank, code, rt, mats, wout_r, wout_b, w_mix, w_hid, jnp.asarray(fold_matrices(), BF))
+    )(todo, feats, rank, code, rt, mats, wout_r, wout_b, w_mix, w_hid, jnp.asarray(fold_matrix(), BF))
 
 
 MESH = pl.DeviceIdType.MESH
 STEPS = (0, -1, 1)
 AROUND = tuple((dx, dy, dz) for dx in STEPS for dy in STEPS for dz in STEPS)[1:]
-
-
-def peer(dx, dy, dz):
-    there = {}
-    for axis, step in (("gx", dx), ("gy", dy), ("gz", dz)):
-        size = lax.axis_size(axis)
-        there[axis] = lax.rem(lax.axis_index(axis) + (step + size), size)
-    return there
-
-
-def greet():
+RING = tuple(v for v in AROUND if v[2] == 0)
+BOTH = ((0, 0, -1), (0, 0, 1))
+
+
+def neighbourhood():
+    axes = []
+    for axis in ("gx", "gy", "gz"):
+        size, me = lax.axis_size(axis), lax.axis_index(axis)
+        axes.append({0: me, -1: lax.rem(me + (size - 1), size), 1: lax.rem(me + 1, size)})
+    return lambda dx, dy, dz: {"gx": axes[0][dx], "gy": axes[1][dy], "gz": axes[2][dz]}
+
+
+def greet(peer, others):
     barrier = pltpu.get_barrier_semaphore()
-    for dx, dy, dz in AROUND:
+    for dx, dy, dz in others:
         pl.semaphore_signal(barrier, inc=1, device_id=peer(dx, dy, dz), device_id_type=MESH)
     return barrier
 
@@ -516,7 +522,8 @@
     w_atom, w_rad, w_hid, w_ten_t, w_mix, neigh, rank, code, rt, todo, mats, wout_r, wout_b,
     rows, rows2, occ_sp, send, recv, inward, outward,
 ):
-    barrier = greet()
+    peer = neighbourhood()
+    barrier = greet(peer, AROUND)
     fetched = [
         pltpu.make_async_copy(far, near, inward.at[j])
         for j, (far, near) in enumerate(
@@ -595,26 +602,38 @@
     return out[0], out[1:]
 
 
-def fold_kernel(grid, out, acc, got, send, recv):
-    barrier = greet()
+def fold_kernel(grid, out, acc, got_x, got_y, got_xy, got_z, send, recv):
+    peer = neighbourhood()
+    barrier = greet(peer, RING + BOTH)
     acc[...] = grid[...]
-    pl.semaphore_wait(barrier, len(AROUND))
-
-    def rim(step, n):
-        return pl.ds(1, n) if step == 0 else pl.ds(0 if step < 0 else n + 1, 1)
-
-    def room(step, n):
-        return pl.ds(0, n if step == 0 else 1)
-
+    pl.semaphore_wait(barrier, len(RING + BOTH))
     copies = []
-    for j, (dx, dy, dz) in enumerate(AROUND):
-        src = acc.at[rim(dx, CX), rim(dy, CY), rim(dz, CZ)]
-        dst = got.at[j, room(dx, CX), room(dy, CY), room(dz, CZ)]
-        copies.append((sent(src, dst, send.at[j], recv.at[j], peer(dx, dy, dz)), dst))
-    for (copy, dst), (dx, dy, dz) in zip(copies, AROUND):
+    for j, (dx, dy, _) in enumerate(RING):
+        if dx and dy:
+            got = got_xy.at[(dx + 1) + (dy + 1) // 2]
+        elif dx:
+            got = got_x.at[(dx + 1) // 2]
+        else:
+            got = got_y.at[(dy + 1) // 2]
+        rim = (
+            pl.ds(1, CX) if dx == 0 else pl.ds(0 if dx < 0 else CX + 1, 1),
+            pl.ds(1, CY) if dy == 0 else pl.ds(0 if dy < 0 else CY + 1, 1),
+        )
+        copies.append((sent(acc.at[rim], got, send.at[j], recv.at[j], peer(dx, dy, 0)), got, dx, dy))
+    for copy, got, dx, dy in copies:
         copy.wait()
-        at = (border(-dx, CX), border(-dy, CY), border(-dz, CZ))
-        acc[at] = acc[at] + dst[...]
+        at = (border(-dx, CX), border(-dy, CY))
+        acc[at] = acc[at] + got[...]
+    inner = (pl.ds(1, CX), pl.ds(1, CY))
+    copies = []
+    for j, (step, rim) in enumerate(((-1, 0), (1, CZ + 1))):
+        copies.append(
+            sent(acc.at[inner + (pl.ds(rim, 1),)], got_z.at[j], send.at[8 + j], recv.at[8 + j], peer(0, 0, step))
+        )
+    for j, step in enumerate((-1, 1)):
+        copies[j].wait()
+        at = inner + (border(-step, CZ),)
+        acc[at] = acc[at] + got_z[j]
     lines = []
     for c in range(CELLS):
         x, y, z = place_of(c)
@@ -634,9 +653,12 @@
         out_specs=vm,
         scratch_shapes=[
             V((EX, EY, EZ, 1, 128), F32),
-            V((len(AROUND), CX, CY, CZ, 1, 128), F32),
-            pltpu.SemaphoreType.DMA((len(AROUND),)),
-            pltpu.SemaphoreType.DMA((len(AROUND),)),
+            V((2, 1, CY, EZ, 1, 128), F32),
+            V((2, CX, 1, EZ, 1, 128), F32),
+            V((4, 1, 1, EZ, 1, 128), F32),
+            V((2, CX, CY, 1, 1, 128), F32),
+            pltpu.SemaphoreType.DMA((10,)),
+            pltpu.SemaphoreType.DMA((10,)),
         ],
         compiler_params=pltpu.CompilerParams(collective_id=1, has_side_effects=True, vmem_limit_bytes=60 * 1024 * 1024),
         name="fold",

time: 58.9 us -> 58.4 us (level)
  no operation moved by 1% of the time
where the time goes in v4:
time: 58.4 us; the launch traced here: 58.1 us
  Pallas kernels  56.1 us (96%)
  local copies, waits for them, and re-layouts  1.42 us (2%)
  between operations  0.66 us (1%)
    pallas_call x1, Pallas kernels, halo_stage(): pl.pallas_call(halo_kernel, out_shape=(jax.ShapeDtypeStruct((EX, EY, EZ,...  21.4 us
    pallas_call x1, Pallas kernels, edge_stage(): pl.pallas_call(edge_kernel, out_shape=(jax.ShapeDtypeStruct((CELLS, 16),...  19.2 us
    pallas_call x1, Pallas kernels, fold_stage(): pl.pallas_call(fold_kernel, out_shape=jax.ShapeDtypeStruct((3, CELLS, 16)...  15.5 us
    unnamed x1, local copies, waits for them, and re-layouts  1.42 us

profile of v4, /device:TPU:1, one launch (start us, length us, event | category | flops | bytes accessed | tf_op | source)
XLA Modules:
  0.0 58.1 jit_solution(1066195867163893944)
XLA Ops:
  0.6 21.4 %halo.1 = (bf16[6,6,4,16,128]{4,3,2,1,0:T(8,128)(2,1)}, s32[32,8,128]{2,1,0:T(8,128)}, s32[32,8,128]{2,1,0:T(8,128)}, bf16[32,48,128]{2,1,0:T(8,128)(2,1)}, s32[...) custom-call(s32[4,2,4]{2,1,0:T(2,128)} %bitcast.19, ...), custom_call_target="tpu_custom_call" | custom-call | tf_op jit(solution)/shard_map/halo/pallas_call | solution.py:581
  22.0 19.2 %edges.1 = (f32[32,16]{1,0:T(8,128)}, f32[144,128]{1,0:T(8,128)}) custom-call(s32[8,256]{1,0:T(8,128)} %get-tuple-element.12.list_s, bf16[144,16,128]{2,1,0:T(8,128)(2,1)} %bitcast.11, s32[32,8,128]{2,1,0:T(8,128)} %get-tuple-element.14.rank_r, s32[32,8,128]{2,1,0:T(8,128)} %get-tuple-element.15.code_r, bf16[32,48,128]{2,1,0:T(8,128)(2,1)} %get-tuple-element.16.rt_r, ...), custom_call_target="tpu_custom_call" | custom-call | tf_op jit(solution)/shard_map/edges/pallas_call | solution.py:452
  41.2 15.5 %fold.1 = f32[3,32,16]{2,1,0:T(8,128)} custom-call(f32[6,6,4,1,128]{4,3,2,1,0:T(1,128)} %bitcast.15), custom_call_target="tpu_custom_call" | custom-call | tf_op jit(solution)/shard_map/fold/pallas_call | solution.py:649
  56.7 1.4 %copy.15 = f32[3,4,4,2,16]{4,3,2,1,0:T(2,128)} copy(f32[3,4,4,2,16]{4,3,2,1,0:T(2,128)} %bitcast.13) | data formatting | bytes 12288

commit v5 on v4

--- a/solution.py
+++ b/solution.py
@@ -12,6 +12,7 @@
 root_three = 1.7320508075688772
 L = 256
 G = 12
+TAIL = 4
 CX, CY, CZ = 4, 4, 2
 EX, EY, EZ = CX + 2, CY + 2, CZ + 2
 CELLS = CX * CY * CZ
@@ -177,7 +178,8 @@
 ):
     fold_copy = pltpu.make_async_copy(fold_h, fold, fold_sem)
     fold_copy.start()
-    groups = lax.div(list_s[2, 0] + (G - 1), G)
+    groups = lax.div(list_s[2, 0] + (G - 1 - TAIL), G)
+    short = lax.min(lax.max(list_s[2, 0] - groups * G, 0), 1)
     ident = eye(128, 128)
     q_sc[...] = jnp.zeros_like(q_sc)
     f_sc[...] = jnp.zeros_like(f_sc)
@@ -187,9 +189,21 @@
     zero = jnp.zeros((16, L), BF)
     centres = 0.5 + 2.0 * iota((8, L), 0, F32)
 
-    def ids_of(gi):
-        ids = [gi * G + i for i in range(G)]
+    def ids_of(gi, count):
+        ids = [gi * G + i for i in range(count)]
         return ids, [list_s[0, i] for i in ids]
+
+    def run(step):
+        def whole(gi, _):
+            step(gi, G)
+            return 0
+
+        def rest(_, none):
+            step(groups, TAIL)
+            return 0
+
+        lax.fori_loop(0, groups, whole, 0)
+        lax.fori_loop(0, short, rest, 0)
 
     def sphere(gi):
         rx, ry, rz = geo_sc[gi, RX], geo_sc[gi, RY], geo_sc[gi, RZ]
@@ -197,8 +211,8 @@
         inv = lax.rsqrt(d2)
         return rx, ry, rz, d2, inv, d2 * inv, rx * inv, ry * inv, rz * inv
 
-    def front(gi, _):
-        ids, cells = ids_of(gi)
+    def front(gi, count):
+        ids, cells = ids_of(gi, count)
         sixteen = iota((16, 128), 0, F32).astype(BF)
         lane_l = iota((16, L), 1)
         unfold = onoff(lax.bitwise_and(lane_l, 15) == iota((16, L), 0)).astype(BF)
@@ -300,17 +314,16 @@
             q_sc[:, c] = q_sc[:, c] + q.reshape(9, 16, 128)
 
         weave(layers(j, i, c) for j, (i, c) in enumerate(zip(ids, cells)))
-        return 0
-
-    lax.fori_loop(0, groups, front, 0)
+
+    run(front)
 
     for m in range(9):
         l = 0 if m == 0 else 1 if m < 4 else 2
         m_sc[m] = nn(q_sc[m].reshape(CELLS * 16, 128).astype(BF), mats[4 + l]).astype(BF).reshape(CELLS, 16, 128)
         q_sc[m] = jnp.zeros((CELLS, 16, 128), F32)
 
-    def middle(gi, _):
-        ids, cells = ids_of(gi)
+    def middle(gi, count):
+        ids, cells = ids_of(gi, count)
         wout_h = jnp.concatenate([(0.5 * wout_b[...]).astype(BF)] * (L // 128), axis=1)
         row = iota((16, 128), 0)
         w_hi = wout_r[0:1, :].astype(BF).astype(F32)
@@ -338,16 +351,15 @@
             en_sc[c] = en_sc[c] + en[0:8]
 
         weave(mix(j, i, c) for j, (i, c) in enumerate(zip(ids, cells)))
-        return 0
-
-    lax.fori_loop(0, groups, middle, 0)
+
+    run(middle)
 
     for m in range(9):
         l = 0 if m == 0 else 1 if m < 4 else 2
         dq_sc[m] = nt(q_sc[m].reshape(CELLS * 16, 128).astype(BF), mats[4 + l]).astype(BF).reshape(CELLS, 16, 128)
 
-    def back(gi, _):
-        ids, cells = ids_of(gi)
+    def back(gi, count):
+        ids, cells = ids_of(gi, count)
         top = jnp.concatenate([w_mix[0:128, :], jnp.zeros((128, 128), BF)], axis=1)
         col, row = iota((16, 256), 1), iota((16, 256), 0)
         part = jnp.where(col < 128, 0, lax.shift_right_logical(col - 128, 4) + 1)
@@ -406,9 +418,8 @@
             f_sc[c] = f_sc[c] + add
 
         weave(scatter(j, i, c) for j, (i, c) in enumerate(zip(ids, cells)))
-        return 0
-
-    lax.fori_loop(0, groups, back, 0)
+
+    run(back)
 
     fold_copy.wait()
 

time: 58.4 us -> 57.2 us (0.979); the launches traced: 58.1 us -> 57.5 us
  Pallas kernels: 56.1 us -> 55.5 us
    pallas_call x1, Pallas kernels: 15.5 us -> 14.9 us  [fold_stage(): pl.pallas_call(fold_kernel, out_shape=jax.ShapeDtypeStruct((3, CELLS, 16)...]
where the time goes in v5:
time: 57.2 us; the launch traced here: 57.5 us
  Pallas kernels  55.5 us (97%)
  local copies, waits for them, and re-layouts  1.42 us (2%)
  between operations  0.66 us (1%)
    pallas_call x1, Pallas kernels, halo_stage(): pl.pallas_call(halo_kernel, out_shape=(jax.ShapeDtypeStruct((EX, EY, EZ,...  21.4 us
    pallas_call x1, Pallas kernels, edge_stage(): pl.pallas_call(edge_kernel, out_shape=(jax.ShapeDtypeStruct((CELLS, 16),...  19.2 us
    pallas_call x1, Pallas kernels, fold_stage(): pl.pallas_call(fold_kernel, out_shape=jax.ShapeDtypeStruct((3, CELLS, 16)...  14.9 us
    unnamed x1, local copies, waits for them, and re-layouts  1.42 us

profile of v5, /device:TPU:1, one launch (start us, length us, event | category | flops | bytes accessed | tf_op | source)
XLA Modules:
  0.0 57.5 jit_solution(12789081079337644559)
XLA Ops:
  0.6 21.4 %halo.1 = (bf16[6,6,4,16,128]{4,3,2,1,0:T(8,128)(2,1)}, s32[32,8,128]{2,1,0:T(8,128)}, s32[32,8,128]{2,1,0:T(8,128)}, bf16[32,48,128]{2,1,0:T(8,128)(2,1)}, s32[...) custom-call(s32[4,2,4]{2,1,0:T(2,128)} %bitcast.19, ...), custom_call_target="tpu_custom_call" | custom-call | tf_op jit(solution)/shard_map/halo/pallas_call | solution.py:592
  22.0 19.2 %edges.1 = (f32[32,16]{1,0:T(8,128)}, f32[144,128]{1,0:T(8,128)}) custom-call(s32[8,256]{1,0:T(8,128)} %get-tuple-element.12.list_s, bf16[144,16,128]{2,1,0:T(8,128)(2,1)} %bitcast.11, s32[32,8,128]{2,1,0:T(8,128)} %get-tuple-element.14.rank_r, s32[32,8,128]{2,1,0:T(8,128)} %get-tuple-element.15.code_r, bf16[32,48,128]{2,1,0:T(8,128)(2,1)} %get-tuple-element.16.rt_r, ...), custom_call_target="tpu_custom_call" | custom-call | tf_op jit(solution)/shard_map/edges/pallas_call | solution.py:463
  41.2 14.9 %fold.1 = f32[3,32,16]{2,1,0:T(8,128)} custom-call(f32[6,6,4,1,128]{4,3,2,1,0:T(1,128)} %bitcast.15), custom_call_target="tpu_custom_call" | custom-call | tf_op jit(solution)/shard_map/fold/pallas_call | solution.py:660
  56.1 1.4 %copy.15 = f32[3,4,4,2,16]{4,3,2,1,0:T(2,128)} copy(f32[3,4,4,2,16]{4,3,2,1,0:T(2,128)} %bitcast.13) | data formatting | bytes 12288

commit v6 on v5

--- a/solution.py
+++ b/solution.py
@@ -12,7 +12,7 @@
 root_three = 1.7320508075688772
 L = 256
 G = 12
-TAIL = 4
+TAIL = 9
 CX, CY, CZ = 4, 4, 2
 EX, EY, EZ = CX + 2, CY + 2, CZ + 2
 CELLS = CX * CY * CZ

time: 57.2 us -> 57.8 us (1.010); the launches traced: 57.5 us -> 57.5 us
    pallas_call x1, Pallas kernels: 19.2 us -> 18.2 us  [edge_stage(): pl.pallas_call(edge_kernel, out_shape=(jax.ShapeDtypeStruct((CELLS, 16),...]
    pallas_call x1, Pallas kernels: 14.9 us -> 15.9 us  [fold_stage(): pl.pallas_call(fold_kernel, out_shape=jax.ShapeDtypeStruct((3, CELLS, 16)...]
where the time goes in v6:
time: 57.8 us; the launch traced here: 57.5 us
  Pallas kernels  55.4 us (96%)
  local copies, waits for them, and re-layouts  1.42 us (2%)
  between operations  0.66 us (1%)
    pallas_call x1, Pallas kernels, halo_stage(): pl.pallas_call(halo_kernel, out_shape=(jax.ShapeDtypeStruct((EX, EY, EZ,...  21.4 us
    pallas_call x1, Pallas kernels, edge_stage(): pl.pallas_call(edge_kernel, out_shape=(jax.ShapeDtypeStruct((CELLS, 16),...  18.2 us
    pallas_call x1, Pallas kernels, fold_stage(): pl.pallas_call(fold_kernel, out_shape=jax.ShapeDtypeStruct((3, CELLS, 16)...  15.9 us
    unnamed x1, local copies, waits for them, and re-layouts  1.42 us

profile of v6, /device:TPU:1, one launch (start us, length us, event | category | flops | bytes accessed | tf_op | source)
XLA Modules:
  0.0 57.5 jit_solution(5988717219777348943)
XLA Ops:
  0.6 21.4 %halo.1 = (bf16[6,6,4,16,128]{4,3,2,1,0:T(8,128)(2,1)}, s32[32,8,128]{2,1,0:T(8,128)}, s32[32,8,128]{2,1,0:T(8,128)}, bf16[32,48,128]{2,1,0:T(8,128)(2,1)}, s32[...) custom-call(s32[4,2,4]{2,1,0:T(2,128)} %bitcast.19, ...), custom_call_target="tpu_custom_call" | custom-call | tf_op jit(solution)/shard_map/halo/pallas_call | solution.py:592
  22.0 18.2 %edges.1 = (f32[32,16]{1,0:T(8,128)}, f32[144,128]{1,0:T(8,128)}) custom-call(s32[8,256]{1,0:T(8,128)} %get-tuple-element.12.list_s, bf16[144,16,128]{2,1,0:T(8,128)(2,1)} %bitcast.11, s32[32,8,128]{2,1,0:T(8,128)} %get-tuple-element.14.rank_r, s32[32,8,128]{2,1,0:T(8,128)} %get-tuple-element.15.code_r, bf16[32,48,128]{2,1,0:T(8,128)(2,1)} %get-tuple-element.16.rt_r, ...), custom_call_target="tpu_custom_call" | custom-call | tf_op jit(solution)/shard_map/edges/pallas_call | solution.py:463
  40.2 15.9 %fold.1 = f32[3,32,16]{2,1,0:T(8,128)} custom-call(f32[6,6,4,1,128]{4,3,2,1,0:T(1,128)} %bitcast.15), custom_call_target="tpu_custom_call" | custom-call | tf_op jit(solution)/shard_map/fold/pallas_call | solution.py:660
  56.1 1.4 %copy.15 = f32[3,4,4,2,16]{4,3,2,1,0:T(2,128)} copy(f32[3,4,4,2,16]{4,3,2,1,0:T(2,128)} %bitcast.13) | data formatting | bytes 12288
